TPU v7x, 512 devices: a whole 4x8x8 slice. The times are simulated.
512 devices in a mesh: walker: 32 (over x, z), tangent: 16 (over y, core).
Axes of the slice: x: 4, y: 8, z: 8, core: 2. Of those that a mesh axis runs over, the one named last changes fastest.
Arguments:
- hidden0: float32 [64, 120, 256], P('walker'), may hold values from -6 to 6
- tangent0: bfloat16 [64, 256, 120, 256], P('walker', 'tangent'), may hold values from -0.5 to 0.5
- laplace0: float32 [64, 120, 256], P('walker'), may hold values from -6 to 6
- spins: int32 [64, 120], P('walker'), may hold values from 0 to 1
- weights: bfloat16 [2, 256, 256], replicated, may hold values from -0.375 to 0.375
- spin_bias: float32 [2, 2, 256], replicated, may hold values from -3 to 3
- readout: float32 [256], replicated, may hold values from -0.03125 to 0.03125
- energy_cotangent: float32 [64], P('walker'), may hold values from -4 to 4
Outputs:
- energy: float32 [64], P('walker')
- grad_weights: float32 [2, 256, 256], P(None, 'tangent')
- grad_bias: float32 [2, 2, 256], replicated
- grad_readout: float32 [256], replicated
All inputs are finite; a program needn't handle non-finite values.
Results may differ from a plain program's by a relative error of at most 0.0094.
Values sent between devices are 32-bit elements; how exact they have to be, the bound alone decides.
No kernel may reach another device: no remote copies, remote signals or barrier semaphores. Data moves between devices by JAX's collectives and lax.ppermute only.
A program may use at most 64 MiB of HBM per device.

v0:
```python
import jax
import jax.numpy as jnp
from jax import lax
from jax.sharding import PartitionSpec as P


def outer(left, right):
    width = right.shape[-1]
    return lax.dot_general(
        left.reshape(-1, left.shape[-1]),
        right.reshape(-1, width),
        (((0,), (0,)), ((), ())),
        preferred_element_type=jnp.float32,
    )


def per_device(hidden0, tangent0, laplace0, spins, weights, spin_bias, readout, energy_cotangent):
    layers = weights.shape[0]
    width = weights.shape[1]
    rows = width // lax.axis_size("tangent")
    offset = lax.axis_index("tangent") * rows
    leading = lax.axis_index("tangent") == 0
    coeff = energy_cotangent / (energy_cotangent.shape[0] * lax.axis_size("walker"))
    hidden, tangents, laplace = (hidden0, tangent0, laplace0)
    stored = []
    for layer in range(layers):
        weight = weights[layer]
        table = spin_bias[layer]
        hid_b = hidden.astype(jnp.bfloat16)
        lap_b = laplace.astype(jnp.bfloat16)
        bias = jnp.where(spins[..., None] == 0, table[0], table[1])
        pre = jnp.dot(hid_b, weight, preferred_element_type=jnp.float32) + bias
        images = jnp.dot(tangents, weight, preferred_element_type=jnp.float32)
        lap_image = jnp.dot(lap_b, weight, preferred_element_type=jnp.float32)
        act = jnp.tanh(pre)
        slope = 1.0 - act * act
        curve = -2.0 * act * slope
        squares = lax.psum(jnp.sum(images * images, axis=1), "tangent")
        kept = images
        stored.append((hid_b, tangents, lap_b, act, slope, curve, kept, lap_image, squares))
        hidden = hidden + act
        laplace = laplace + slope * lap_image + curve * squares
        tangents = (tangents.astype(jnp.float32) + slope[:, None] * images).astype(jnp.bfloat16)
    tang_f = tangents.astype(jnp.float32)
    grads_t = jnp.sum(tang_f * readout, axis=(2, 3))
    lap_val = jnp.sum(laplace * readout, axis=(1, 2))
    norm_total = lax.psum(jnp.sum(grads_t * grads_t, axis=1), "tangent")
    energy = -0.5 * (lap_val + norm_total)
    scaled = coeff[:, None] * grads_t
    shared_read = -0.5 * jnp.sum(coeff[:, None, None] * laplace, axis=(0, 1))
    own_read = -jnp.sum(scaled[:, :, None, None] * tang_f, axis=(0, 1, 2))
    g_lap = -0.5 * coeff[:, None, None] * jnp.ones_like(laplace) * readout
    g_tan = -scaled[:, :, None, None] * readout
    g_hid = jnp.zeros_like(hidden)
    grad_w = [None] * layers
    grad_b = [None] * layers
    for layer in reversed(range(layers)):
        hid_b, tang_in, lap_b, act, slope, curve, kept, lap_image, squares = stored[layer]
        weight = weights[layer]
        images = kept
        g_lap_image = slope * g_lap
        g_images = slope[:, None] * g_tan + 2.0 * (curve * g_lap)[:, None] * images
        crossed = lax.psum(jnp.sum(g_tan * images, axis=1), "tangent")
        g_slope = g_lap * lap_image + crossed
        g_act = -2.0 * act * g_slope + (6.0 * act * act - 2.0) * g_lap * squares + g_hid
        g_pre = g_act * slope
        g_pre_b = g_pre.astype(jnp.bfloat16)
        g_images_b = g_images.astype(jnp.bfloat16)
        g_lap_image_b = g_lap_image.astype(jnp.bfloat16)
        tang_flat = tang_in.reshape(-1, width)
        grad_flat = g_images_b.reshape(-1, width)
        hid_cols = lax.dynamic_slice_in_dim(hid_b, offset, rows, 2)
        lap_cols = lax.dynamic_slice_in_dim(lap_b, offset, rows, 2)
        own_rows = outer(hid_cols, g_pre_b) + outer(lap_cols, g_lap_image_b)
        share = (
            lax.psum_scatter(
                outer(tang_flat, grad_flat), "tangent", scatter_dimension=0, tiled=True
            )
            + own_rows
        )
        grad_w[layer] = lax.psum(share, "walker")
        first_spin = jnp.sum(jnp.where(spins[..., None] == 0, g_pre, 0.0), axis=(0, 1))
        second_spin = jnp.sum(jnp.where(spins[..., None] == 1, g_pre, 0.0), axis=(0, 1))
        grad_b[layer] = jnp.stack([first_spin, second_spin])
        if layer > 0:
            g_hid = jnp.dot(g_pre_b, weight.T, preferred_element_type=jnp.float32)
            g_tan = g_tan + jnp.dot(g_images_b, weight.T, preferred_element_type=jnp.float32)
            g_lap = g_lap + jnp.dot(g_lap_image_b, weight.T, preferred_element_type=jnp.float32)
    grad_weights = jnp.stack(grad_w)
    bias_term = jnp.where(leading, jnp.stack(grad_b), 0.0)
    read_term = own_read + jnp.where(leading, shared_read, 0.0)
    grad_bias, grad_readout = lax.psum((bias_term, read_term), ("walker", "tangent"))
    return (energy, grad_weights, grad_bias, grad_readout)


def solution(mesh):
    in_specs = (
        P("walker", None, None),
        P("walker", "tangent", None, None),
        P("walker", None, None),
        P("walker", None),
        P(),
        P(),
        P(),
        P("walker"),
    )
    out_specs = (P("walker"), P(None, "tangent", None), P(), P())
    return jax.shard_map(
        per_device, mesh=mesh, in_specs=in_specs, out_specs=out_specs, check_vma=False
    )
```

profile of v0, /device:TPU:32, one launch (start us, length us, event | category | flops | bytes accessed | tf_op | source)
XLA Modules:
  0.0 413.7 jit_solution(17406518419715906581)
XLA Ops:
  7.2 0.7 broadcast_compare_fusion
  7.9 0.7 broadcast_multiply_fusion.3
  8.6 0.8 fusion.68
  9.3 1.3 add_convert_fusion.7
  10.7 3.0 add_convert_fusion.3
  14.0 2.5 fusion
  16.7 4.9 %multiply_reduce_fusion.1 = (f32[2,120,256]{2,1,0:T(8,128)}, f32[2,120,256]{2,1,0:T(8,128)}, f32[2,120,256]{2,1,0:T(8,128)}, f32[2,120,256]{2,1,0:T(8,128)}, f32[2,16,120,256]{3,2,1,0:T(8,128)}) fusion(f32[2,16,120,256]{3,2,1,0:T(8,128)S(1)} %get-tuple-element.54, f32[2,16,256]{2,1,0:T(8,128)S(1)} %broadcast_multiply_fusion, ...), kind=kOutput, calls=%fused_computation.5 | convolution fusion | flops 515850240 | bytes 17399808 | tf_op jit(solution)/shard_map/dot_general | solution.py:87
  21.6 3.6 convolution_bitcast_fusion
  25.3 1.7 convert_element_type.45
  27.1 1.6 convert_element_type.46
  28.9 23.6 %psum.65 = f32[2]{0:T(128)S(1)} all-reduce(f32[2]{0:T(128)S(1)} %get-tuple-element.49), channel_id=1, replica_groups=mesh['walker'=32,'tangent'=16] {'tangent'}, use_global_device_ids=true, to_apply=%region_7.8 | all-reduce | flops 2 | bytes 16 | tf_op jit(solution)/shard_map/psum | solution.py:47
  52.5 2.3 fusion.1
  54.8 86.1 %all-reduce.5.cloned.1.call-done = (f32[2,120,256]{2,1,0:T(8,128)}, f32[2,120,256]{2,1,0:T(8,128)}, f32[2,120,256]{2,1,0:T(8,128)}, f32[2,120,256]{2,1,0:T(8,128)}) async-done(((f32[2,120,256]{2,1,0:T(8,128)}, f32[2,120,256]{2,1,0:T(8,128)}, f32[2,120,256]{2,1,0:T(8,128)}, f32[2,120,256]{2,1,0:T(8,128)}), (f32[2,120,256]{2,1,0:T(8,128)}, f32[2,120,256]{2,1,0:T(8,128)}, f32[2,120,256]{2,1,0:T(8,128)}, ...) | async-done | bytes 983056 | tf_op jit(solution)/shard_map/psum | solution.py:38
  140.9 2.1 fusion.66
  143.0 5.1 %fusion.6 = f32[256,256]{0,1:T(8,128)} fusion(bf16[2,16,120,256]{3,2,1,0:T(8,128)(2,1)S(1)} %copy-done.2, f32[2,16,120,256]{3,2,1,0:T(8,128)} %copy-done.1, f32[2,16,120,256]{3,2,1,0:T(8,128)} %get-tuple-element.57, f32[2,120,256]{2,1,0:T(8,128)S(1)} %get-tuple-element.38, f32[2,16,256]{2,1,0:T(8,128)S(1)} %broadcast_multiply_fusion, ...), kind=kOutput, calls=%fused_computation.16 | convolution fusion | flops 508231680 | bytes 10616832 | tf_op jit(solution)/shard_map/dot_general | solution.py:9
  148.1 1.8 copy.49
  149.9 1.4 fusion.26
  151.5 1.5 select_reduce_fusion.1
  153.3 102.0 %all-reduce = (f32[2,2,256]{2,1,0:T(2,128)}, f32[256]{0:T(256)}) all-reduce(f32[2,2,256]{2,1,0:T(2,128)S(1)} %maximum_select_fusion, f32[256]{0:T(256)S(1)} %select_add_fusion), channel_id=1, replica_groups=mesh['walker'=32,'tangent'=16] {'walker','tangent'}, use_global_device_ids=true, to_apply=%region_20.21 | all-reduce | flops 1280 | bytes 10240 | tf_op jit(solution)/shard_map/psum | solution.py:92
  256.0 1.0 fusion.12
  257.0 5.1 %reduce-scatter.7.cloned.1.call-done = f32[16,256]{1,0:T(8,128)} async-done(((f32[256,256]{1,0:T(8,128)}), f32[16,256]{1,0:T(8,128)}) %reduce-scatter.7.cloned.1.call-update) | async-done | bytes 16400 | tf_op jit(solution)/shard_map/reduce_scatter | solution.py:76
  262.1 1.0 fusion.15
  263.1 143.5 %all-reduce.1 = (f32[1,16,256]{2,1,0:T(8,128)S(1)}, f32[1,16,256]{2,1,0:T(8,128)S(1)}) all-reduce(f32[1,16,256]{2,1,0:T(8,128)S(1)} %fusion.12, f32[1,16,256]{2,1,0:T(8,128)S(1)} %fusion.15), channel_id=1, replica_groups=mesh['walker'=32,'tangent'=16] {'walker'}, use_global_device_ids=true, to_apply=%region_15.16 | all-reduce | flops 8192 | bytes 65536 | tf_op jit(solution)/shard_map/psum | solution.py:81
  406.5 0.6 pad_maximum_fusion
  (38 shorter events, 2.0 us)
Async XLA Ops:
  7.2 133.7 %all-reduce.5.cloned.1.call-start = ((), (), s32[]{:S(2)}) async-start(), calls=%async_computation.4 | async-start | bytes 1966080 | tf_op jit(solution)/shard_map/psum | solution.py:38
  10.7 3.0 copy-start.4
  10.7 3.0 copy-start.3
  10.7 3.0 copy-start.9
  13.7 3.0 copy-start.1
  16.5 5.1 %copy-start = (f32[2,16,120,256]{3,2,1,0:T(8,128)}, f32[2,16,120,256]{3,2,1,0:T(8,128)S(1)}, u32[]{:S(2)}) copy-start(f32[2,16,120,256]{3,2,1,0:T(8,128)S(1)} %get-tuple-element.56) | copy-start | bytes 11796484
  21.6 234.4 %reduce-scatter.9.cloned.1.call-start = ((), (), s32[]{:S(2)}) async-start(), calls=%async_computation.3 | async-start | bytes 278528 | tf_op jit(solution)/shard_map/reduce_scatter | solution.py:76
  25.3 117.8 %copy-start.2 = (bf16[2,16,120,256]{3,2,1,0:T(8,128)(2,1)S(1)}, bf16[2,16,120,256]{3,2,1,0:T(8,128)(2,1)}, u32[]{:S(2)}) copy-start(bf16[2,16,120,256]{3,2,1,0:T(8,128)(2,1)} %param.9) | copy-start | bytes 5898244
  25.3 236.8 %reduce-scatter.7.cloned.1.call-start = ((), (), s32[]{:S(2)}) async-start(), calls=%async_computation.2 | async-start | bytes 278528 | tf_op jit(solution)/shard_map/reduce_scatter | solution.py:76
  148.1 4.9 %copy-start.7 = (bf16[2,120,256]{2,1,0:T(8,128)(2,1)S(1)}, bf16[2,120,256]{2,1,0:T(8,128)(2,1)}, u32[]{:S(2)}) copy-start(bf16[2,120,256]{2,1,0:T(8,128)(2,1)} %convert_element_type.45) | copy-start | bytes 368644
  148.1 107.2 %copy-start.5 = (bf16[2,120,256]{2,1,0:T(8,128)(2,1)S(1)}, bf16[2,120,256]{2,1,0:T(8,128)(2,1)}, u32[]{:S(2)}) copy-start(bf16[2,120,256]{2,1,0:T(8,128)(2,1)} %copy-done.4) | copy-start | bytes 368644
  148.1 107.9 %copy-start.6 = (bf16[2,120,256]{2,1,0:T(8,128)(2,1)S(1)}, bf16[2,120,256]{2,1,0:T(8,128)(2,1)}, u32[]{:S(2)}) copy-start(bf16[2,120,256]{2,1,0:T(8,128)(2,1)} %get-tuple-element.30) | copy-start | bytes 368644
  148.1 114.0 %copy-start.8 = (bf16[2,120,256]{2,1,0:T(8,128)(2,1)S(1)}, bf16[2,120,256]{2,1,0:T(8,128)(2,1)}, u32[]{:S(2)}) copy-start(bf16[2,120,256]{2,1,0:T(8,128)(2,1)} %convert_element_type.46) | copy-start | bytes 368644
Sparse Core Ops, SparseCore 0:
  21.7 119.1 all-reduce.4
  143.9 58.0 reduce-scatter.8
  204.8 57.2 reduce-scatter.6
where the time goes:
time: 414 us
  blocking collectives  269 us (65%)
  waiting for transfers between devices  91.2 us (22%)
  matrix products  28.3 us (7%)
  between operations  13.9 us (3%)
  other arithmetic  8.45 us (2%)
    psum x1, blocking collectives, per_device(): grad_w[layer] = lax.psum(share, 'walker')  143 us
    psum x1, blocking collectives, per_device(): lax.psum((bias_term, read_term), ('walker', 'tangent'))  102 us
    psum x1, waiting for transfers between devices, per_device(): squares = lax.psum(jnp.sum(images * images, axis=1), 'tangent')  86.1 us
    psum x1, blocking collectives, per_device(): norm_total = lax.psum(jnp.sum(grads_t * grads_t, axis=1), 'tangent')  23.6 us
    dot_general x6, matrix products, outer(): lax.dot_general(left.reshape(-1, left.shape[-1]), right.reshape(-1, width...  11.1 us
  transfers between devices with their start and end apart: 3, of which 2 were waited for; matrix products, arithmetic and copies ran while one was open for 6% of the time, Pallas kernels for 0%

commit v1 on v0

v1 whole, which is shorter than its diff:
```python
import functools

import jax
import jax.numpy as jnp
from jax import lax
from jax.experimental import pallas as pl
from jax.experimental.pallas import tpu as pltpu
from jax.sharding import Mesh, PartitionSpec as P

NX, NZ, NY, NC = 4, 8, 8, 2
GROUP = NY * NC
CHUNK = 4
F32 = jnp.float32
BF16 = jnp.bfloat16


def mm(a, b):
    return lax.dot_general(a, b, (((1,), (0,)), ((), ())), preferred_element_type=F32)


def outer(a, b):
    return lax.dot_general(a, b, (((0,), (0,)), ((), ())), preferred_element_type=F32)


def local_kernel(cot_ref, tan_ref, hid_ref, lap_ref, spin_ref, w_ref, bias_ref, read_ref, out_ref,
                 wt_ref, a0_ref, a1_ref, s0_ref, s1_ref, amp1_ref, b1_ref, b0_ref, gl1_ref, h1_ref,
                 sq0_ref, sq1_ref, x0_ref, x1_ref, gw_ref, acc_ref, *, walkers, ne, width, walkers_all):
    w = pl.program_id(0)
    k = pl.program_id(1)
    rows = walkers * ne
    read = read_ref[...]

    def coeff(i):
        return cot_ref[i] * (1.0 / walkers_all)

    @pl.when((w == 0) & (k == 0))
    def _():
        wt_ref[...] = w_ref[1].T
        spin = spin_ref[...]
        hid0 = hid_ref[...]

        def layer(hid, l):
            bias = jnp.where(spin == 0, bias_ref[l, 0:1, :], bias_ref[l, 1:2, :])
            return jnp.tanh(mm(hid.astype(BF16), w_ref[l]) + bias)

        a0 = layer(hid0, 0)
        h1 = hid0 + a0
        a1 = layer(h1, 1)
        a0_ref[...] = a0
        a1_ref[...] = a1
        h1_ref[...] = h1.astype(BF16)
        s0 = 1.0 - a0 * a0
        s1 = 1.0 - a1 * a1
        s0_ref[...] = s0
        s1_ref[...] = s1
        cr = jnp.concatenate([jnp.broadcast_to(coeff(i) * read, (ne, width)) for i in range(walkers)], axis=0)
        gl2 = -0.5 * cr
        amp1_ref[...] = -cr * s1
        b1_ref[...] = 2.0 * cr * a1 * s1
        gl1 = gl2 + mm((s1 * gl2).astype(BF16), wt_ref[...])
        gl1_ref[...] = gl1
        b0_ref[...] = -4.0 * a0 * s0 * gl1
        sq0_ref[...] = jnp.zeros_like(sq0_ref)
        sq1_ref[...] = jnp.zeros_like(sq1_ref)
        x0_ref[...] = jnp.zeros_like(x0_ref)
        x1_ref[...] = jnp.zeros_like(x1_ref)
        gw_ref[...] = jnp.zeros_like(gw_ref)
        acc_ref[...] = jnp.zeros_like(acc_ref)

    c = coeff(w)
    here = pl.ds(pl.multiple_of(w * ne, 8), ne)
    s0 = s0_ref[here]
    s1 = s1_ref[here]
    tan0 = tan_ref[...]

    def split(v):
        return v.reshape(CHUNK, ne, width)

    def flat(v):
        return v.reshape(CHUNK * ne, width)

    z0 = split(mm(tan0, w_ref[0]))
    sq0_ref[here] += jnp.sum(z0 * z0, axis=0)
    tan1 = flat(split(tan0.astype(F32)) + s0[None] * z0).astype(BF16)
    z1 = split(mm(tan1, w_ref[1]))
    sq1_ref[here] += jnp.sum(z1 * z1, axis=0)
    tan2 = split(tan1.astype(F32)) + s1[None] * z1
    tan2 = tan2.astype(BF16).astype(F32)
    cols = jnp.sum(tan2, axis=1)
    g = jnp.sum(cols * read, axis=1, keepdims=True)
    acc_ref[pl.ds(w, 1), 0:1, :] += jnp.broadcast_to(jnp.sum(g * g, axis=0, keepdims=True), (1, width))[None]
    acc_ref[pl.ds(w, 1), 1:2, :] += jnp.sum(g * cols, axis=0, keepdims=True)[None]
    gt = g[:, :, None]
    x1_ref[here] += jnp.sum(gt * z1, axis=0)
    gz1 = flat(gt * amp1_ref[here][None] + b1_ref[here][None] * z1).astype(BF16)
    gw_ref[1] += outer(tan1, gz1)
    gt1 = split(mm(gz1, wt_ref[...])) - (c * gt) * read[None]
    x0_ref[here] += jnp.sum(gt1 * z0, axis=0)
    gz0 = flat(s0[None] * gt1 + b0_ref[here][None] * z0).astype(BF16)
    gw_ref[0] += outer(tan0, gz0)

    @pl.when((w == pl.num_programs(0) - 1) & (k == pl.num_programs(1) - 1))
    def _():
        share = 1.0 / GROUP
        spin = spin_ref[...]
        cr = jnp.concatenate([jnp.broadcast_to(coeff(i) * read, (ne, width)) for i in range(walkers)], axis=0)
        gl2 = -0.5 * cr
        a0, a1, s0, s1, gl1 = a0_ref[...], a1_ref[...], s0_ref[...], s1_ref[...], gl1_ref[...]
        sq0, sq1 = sq0_ref[...], sq1_ref[...]
        lap0 = lap_ref[...]
        lb0 = lap0.astype(BF16)
        lz0 = mm(lb0, w_ref[0])
        lap1 = share * (lap0 + s0 * lz0) - 2.0 * a0 * s0 * sq0
        lb1 = lap1.astype(BF16)
        lz1 = mm(lb1, w_ref[1])
        lap2 = lap1 + s1 * lz1 - 2.0 * a1 * s1 * sq1
        glz1 = (s1 * gl2).astype(BF16)
        glz0 = (s0 * gl1).astype(BF16)
        gs1 = gl2 * lz1 - cr * x1_ref[...]
        gz1 = (-2.0 * a1 * gs1 + (6.0 * a1 * a1 - 2.0) * gl2 * sq1) * s1
        gz1b = gz1.astype(BF16)
        gw1 = gw_ref[1] + outer(h1_ref[...], gz1b) + outer(lb1, glz1)
        gh1 = mm(gz1b, wt_ref[...])
        gs0 = gl1 * (share * lz0) + x0_ref[...]
        gz0 = (-2.0 * a0 * gs0 + (6.0 * a0 * a0 - 2.0) * gl1 * sq0 + gh1) * s0
        gw0 = gw_ref[0] + outer(hid_ref[...].astype(BF16), gz0.astype(BF16)) + share * outer(lb0, glz0)
        block = width // GROUP
        for y in range(NY):
            for core in range(NC):
                at = (y * NC + core) * block
                base = 2 * block * y
                out_ref[core, base:base + block, :] = gw0[at:at + block]
                out_ref[core, base + block:base + 2 * block, :] = gw1[at:at + block]
        lapsum = jnp.sum(lap2.reshape(walkers, ne, width), axis=1)
        small = []
        for gz in (gz0, gz1):
            for s in range(2):
                small.append(jnp.sum(jnp.where(spin == s, gz, 0.0), axis=0, keepdims=True))
        gread = jnp.zeros((1, width), F32)
        lane = lax.broadcasted_iota(jnp.int32, (1, width), 1)
        energy = jnp.zeros((1, width), F32)
        for i in range(walkers):
            gread -= coeff(i) * (0.5 * lapsum[i:i + 1] + acc_ref[i, 1:2, :])
            e = -0.5 * (jnp.sum(lapsum[i:i + 1] * read, axis=1, keepdims=True) + acc_ref[i, 0:1, :])
            energy = jnp.where(lane == i, e, energy)
        tail = jnp.concatenate(small + [gread, energy, jnp.zeros((2, width), F32)], axis=0)
        for core in range(NC):
            out_ref[core, 2 * block * NY:, :] = tail


def local_part(hidden0, tangent0, laplace0, spins, weights, spin_bias, readout, cot):
    walkers, tangents, ne, width = tangent0.shape
    rows = walkers * ne
    steps = tangents // CHUNK
    body = functools.partial(local_kernel, walkers=walkers, ne=ne, width=width,
                             walkers_all=walkers * NX * NZ)
    full = lambda *shape: pl.BlockSpec(shape, lambda w, k: (0,) * len(shape))
    wide = pltpu.VMEM((rows, width), F32)
    return pl.pallas_call(
        body,
        grid=(walkers, steps),
        out_shape=jax.ShapeDtypeStruct((NC, width + 8, width), F32),
        in_specs=[
            pl.BlockSpec(memory_space=pltpu.SMEM),
            pl.BlockSpec((CHUNK * ne, width), lambda w, k: (w * steps + k, 0)),
            full(rows, width),
            full(rows, width),
            full(rows, 1),
            full(2, width, width),
            full(2, 2, width),
            full(1, width),
        ],
        out_specs=full(NC, width + 8, width),
        scratch_shapes=[pltpu.VMEM((width, width), BF16)] + [wide] * 8 + [pltpu.VMEM((rows, width), BF16)]
        + [wide] * 4 + [pltpu.VMEM((2, width, width), F32), pltpu.VMEM((walkers, 8, width), F32)],
        compiler_params=pltpu.CompilerParams(vmem_limit_bytes=48 * 1024 * 1024),
        name="local_part",
    )(cot, tangent0.reshape(-1, width), hidden0.reshape(rows, width), laplace0.reshape(rows, width),
      spins.reshape(rows, 1), weights, spin_bias, readout.reshape(1, width))


def per_device(hidden0, tangent0, laplace0, spins, weights, spin_bias, readout, energy_cotangent):
    walkers = hidden0.shape[0]
    width = weights.shape[1]
    block = 2 * width // GROUP
    part = local_part(hidden0, tangent0, laplace0, spins, weights, spin_bias, readout, energy_cotangent)
    part = jnp.sum(lax.all_to_all(part, "core", 0, 0), axis=0)
    tail = jnp.broadcast_to(part[None, width:], (NY, 8, width))
    part = jnp.concatenate([part[:width].reshape(NY, block, width), tail], axis=1)
    part = jnp.sum(lax.all_to_all(part, "y", 0, 0), axis=0)
    energy = part[block + 5, :walkers]
    for axis, size in (("x", NX), ("z", NZ)):
        part = jnp.broadcast_to(part[None], (size,) + part.shape)
        part = jnp.sum(lax.all_to_all(part, axis, 0, 0), axis=0)
    grad_weights = part[:block].reshape(2, block // 2, width)
    grad_bias = part[block:block + 4].reshape(2, 2, width)
    return energy, grad_weights, grad_bias, part[block + 4]


def solution(mesh):
    split = Mesh(mesh.devices.reshape(NX, NZ, NY, NC), ("x", "z", "y", "core"))
    walker, tangent = ("x", "z"), ("y", "core")
    in_specs = (
        P(walker, None, None),
        P(walker, tangent, None, None),
        P(walker, None, None),
        P(walker, None),
        P(),
        P(),
        P(),
        P(walker),
    )
    out_specs = (P(walker), P(None, tangent, None), P(), P())
    return jax.shard_map(
        per_device, mesh=split, in_specs=in_specs, out_specs=out_specs, check_vma=False
    )
```

time: 414 us -> 77 us (0.19)
  the two profiles are of different devices: /device:TPU:32 before, /device:TPU:8 now
where the time goes in v1:
time: 77 us; the launch traced here: 76.4 us
  blocking collectives  33.9 us (44%)
  waiting for transfers between devices  10.7 us (14%)
  Pallas kernels  10.4 us (14%)
  local copies, waits for them, and re-layouts  10.3 us (13%)
  starting transfers between devices  10.3 us (13%)
    all_to_all x1, blocking collectives, per_device(): part = jnp.sum(lax.all_to_all(part, 'y', 0, 0), axis=0)  20.6 us
    all_to_all x1, waiting for transfers between devices, per_device(): part = jnp.sum(lax.all_to_all(part, axis, 0, 0), axis=0)  10.7 us
    pallas_call x1, Pallas kernels, local_part(): pl.pallas_call(body, grid=(walkers, steps), out_shape=jax.ShapeDtypeStruc...  10.4 us
    all_to_all x1, starting transfers between devices, per_device(): part = jnp.sum(lax.all_to_all(part, axis, 0, 0), axis=0)  10.3 us
    all_to_all x1, blocking collectives, per_device(): part = jnp.sum(lax.all_to_all(part, axis, 0, 0), axis=0)  9.11 us
    unnamed x14, local copies, waits for them, and re-layouts  6.4 us
    all_to_all x1, blocking collectives, per_device(): part = jnp.sum(lax.all_to_all(part, 'core', 0, 0), axis=0)  4.14 us
  transfers between devices with their start and end apart: 1, of which 1 were waited for; matrix products, arithmetic and copies ran while one was open for 1% of the time, Pallas kernels for 0%

profile of v1, /device:TPU:8, one launch (start us, length us, event | category | flops | bytes accessed | tf_op | source)
XLA Modules:
  0.0 76.4 jit_solution(5135165118778431292)
XLA Ops:
  0.6 0.9 %reshape.43.spin_ref = s32[240,1]{1,0:T(8,128)S(1)} reshape(s32[2,120]{1,0:T(2,128)} %param.11) | data formatting | bytes 1920 | tf_op jit(solution)/shard_map/reshape | solution.py:179
  1.5 0.0 copy-start
  1.5 1.5 %copy-done = bf16[2,16,120,256]{3,2,1,0:T(8,128)(2,1)S(1)} copy-done((bf16[2,16,120,256]{3,2,1,0:T(8,128)(2,1)S(1)}, bf16[2,16,120,256]{3,2,1,0:T(8,128)(2,1)}, u32[]{:S(2)}) %copy-start) | copy-done | bytes 1966104
  3.1 0.0 copy-start.1
  3.1 0.9 %copy-done.1 = bf16[2,256,256]{2,1,0:T(8,128)(2,1)S(1)} copy-done((bf16[2,256,256]{2,1,0:T(8,128)(2,1)S(1)}, bf16[2,256,256]{2,1,0:T(8,128)(2,1)}, u32[]{:S(2)}) %copy-start.1) | copy-done | bytes 262168
  4.0 0.0 copy-start.2
  4.0 0.9 %copy-done.2 = f32[2,120,256]{2,1,0:T(8,128)S(1)} copy-done((f32[2,120,256]{2,1,0:T(8,128)S(1)}, f32[2,120,256]{2,1,0:T(8,128)}, u32[]{:S(2)}) %copy-start.2) | copy-done | bytes 245784
  5.0 0.0 copy-start.3
  5.0 0.9 %copy-done.3 = f32[2,120,256]{2,1,0:T(8,128)S(1)} copy-done((f32[2,120,256]{2,1,0:T(8,128)S(1)}, f32[2,120,256]{2,1,0:T(8,128)}, u32[]{:S(2)}) %copy-start.3) | copy-done | bytes 245784
  5.9 0.0 copy-start.4
  5.9 0.7 copy-done.4
  6.6 0.7 copy-done.5
  7.3 0.7 copy-done.6
  7.9 10.4 %local_part.1 = f32[2,264,256]{2,1,0:T(8,128)S(1)} custom-call(f32[2]{0:T(128)S(1)} %copy-done.6, bf16[3840,256]{1,0:T(8,128)(2,1)S(1)} %bitcast.9, f32[240,256]{1,0:T(8,128)S(1)} %bitcast.10, f32[240,256]{1,0:T(8,128)S(1)} %bitcast.11, s32[240,1]{1,0:T(8,128)S(1)} %reshape.43.spin_ref, bf16[2,256,256]{2,1,0:T(8,128)(2,1)S(1)} %copy-done.1, ...), custom_call_target="tpu_custom_call" | custom-call | tf_op jit(solution)/shard_map/local_part/pallas_call | solution.py:159
  18.3 4.1 %all_to_all.20 = f32[2,264,256]{2,1,0:T(8,128)S(1)} all-to-all(f32[2,264,256]{2,1,0:T(8,128)S(1)} %local_part.1), channel_id=1, replica_groups=mesh['x'=4,'z'=8,'y'=8,'core'=2] {'core'}, dimensions={0} | all-to-all | bytes 1081344 | tf_op jit(solution)/shard_map/all_to_all | solution.py:187
  22.6 20.6 %all_to_all.21 = f32[8,40,256]{2,1,0:T(8,128)S(1)} all-to-all(f32[8,40,256]{2,1,0:T(8,128)S(1)} %pad_maximum_fusion), channel_id=1, replica_groups=mesh['x'=4,'z'=8,'y'=8,'core'=2] {'y'}, dimensions={0} | all-to-all | bytes 655360 | tf_op jit(solution)/shard_map/all_to_all | solution.py:190
  43.3 9.1 %all_to_all.22 = f32[4,40,256]{2,1,0:T(8,128)S(1)} all-to-all(f32[4,40,256]{2,1,0:T(8,128)S(1)} %broadcast_in_dim.7), channel_id=1, replica_groups=mesh['x'=4,'z'=8,'y'=8,'core'=2] {'x'}, dimensions={0} | all-to-all | bytes 327680 | tf_op jit(solution)/shard_map/all_to_all | solution.py:194
  52.4 0.7 broadcast_in_dim.8
  53.1 10.3 %all-to-all-start.3 = ((f32[8,40,256]{2,1,0:T(8,128)}), f32[8,40,256]{2,1,0:T(8,128)S(1)}, u32[]{:S(2)}, u32[]{:S(2)}) async-start(f32[8,40,256]{2,1,0:T(8,128)} %broadcast_in_dim.8), calls=%async_computation.3 | async-start | bytes 655360 | tf_op jit(solution)/shard_map/all_to_all | solution.py:194
  63.4 0.5 slice_bitcast_fusion
  64.0 10.7 %all-to-all-done.3 = f32[8,40,256]{2,1,0:T(8,128)S(1)} async-done(((f32[8,40,256]{2,1,0:T(8,128)}), f32[8,40,256]{2,1,0:T(8,128)S(1)}, u32[]{:S(2)}, u32[]{:S(2)}) %all-to-all-start.3) | async-done | bytes 327712 | tf_op jit(solution)/shard_map/all_to_all | solution.py:194
  74.6 0.6 slice.29
  75.2 0.6 slice.27
  75.8 0.6 reshape.42
  (12 shorter events, 0.2 us)
Async XLA Ops:
  1.5 1.6 %copy-start = (bf16[2,16,120,256]{3,2,1,0:T(8,128)(2,1)S(1)}, bf16[2,16,120,256]{3,2,1,0:T(8,128)(2,1)}, u32[]{:S(2)}) copy-start(bf16[2,16,120,256]{3,2,1,0:T(8,128)(2,1)} %param.9) | copy-start | bytes 5898244
  3.1 0.9 %copy-start.1 = (bf16[2,256,256]{2,1,0:T(8,128)(2,1)S(1)}, bf16[2,256,256]{2,1,0:T(8,128)(2,1)}, u32[]{:S(2)}) copy-start(bf16[2,256,256]{2,1,0:T(8,128)(2,1)} %w_ref.1) | copy-start | bytes 786436
  4.0 0.9 %copy-start.2 = (f32[2,120,256]{2,1,0:T(8,128)S(1)}, f32[2,120,256]{2,1,0:T(8,128)}, u32[]{:S(2)}) copy-start(f32[2,120,256]{2,1,0:T(8,128)} %param.8) | copy-start | bytes 737284
  5.0 0.9 %copy-start.3 = (f32[2,120,256]{2,1,0:T(8,128)S(1)}, f32[2,120,256]{2,1,0:T(8,128)}, u32[]{:S(2)}) copy-start(f32[2,120,256]{2,1,0:T(8,128)} %param.10) | copy-start | bytes 737284
  5.9 0.7 copy-start.4
  6.6 0.7 copy-start.5
  7.3 0.7 copy-start.6
  53.1 21.5 %all-to-all-start.3 = ((f32[8,40,256]{2,1,0:T(8,128)}), f32[8,40,256]{2,1,0:T(8,128)S(1)}, u32[]{:S(2)}, u32[]{:S(2)}) async-start(f32[8,40,256]{2,1,0:T(8,128)} %broadcast_in_dim.8), calls=%async_computation.3 | async-start | bytes 655360 | tf_op jit(solution)/shard_map/all_to_all | solution.py:194

commit v2 on v1

--- a/solution.py
+++ b/solution.py
@@ -9,7 +9,7 @@
 
 NX, NZ, NY, NC = 4, 8, 8, 2
 GROUP = NY * NC
-CHUNK = 4
+CHUNK = 16
 F32 = jnp.float32
 BF16 = jnp.bfloat16
 
@@ -33,10 +33,14 @@
     def coeff(i):
         return cot_ref[i] * (1.0 / walkers_all)
 
+    def spin_column():
+        turned = spin_ref[...].astype(F32).T
+        return jnp.concatenate([turned[:, i:i + 1] for i in range(walkers)], axis=0)
+
     @pl.when((w == 0) & (k == 0))
     def _():
         wt_ref[...] = w_ref[1].T
-        spin = spin_ref[...]
+        spin = spin_column()
         hid0 = hid_ref[...]
 
         def layer(hid, l):
@@ -102,7 +106,7 @@
     @pl.when((w == pl.num_programs(0) - 1) & (k == pl.num_programs(1) - 1))
     def _():
         share = 1.0 / GROUP
-        spin = spin_ref[...]
+        spin = spin_column()
         cr = jnp.concatenate([jnp.broadcast_to(coeff(i) * read, (ne, width)) for i in range(walkers)], axis=0)
         gl2 = -0.5 * cr
         a0, a1, s0, s1, gl1 = a0_ref[...], a1_ref[...], s0_ref[...], s1_ref[...], gl1_ref[...]
@@ -165,7 +169,7 @@
             pl.BlockSpec((CHUNK * ne, width), lambda w, k: (w * steps + k, 0)),
             full(rows, width),
             full(rows, width),
-            full(rows, 1),
+            full(walkers, ne),
             full(2, width, width),
             full(2, 2, width),
             full(1, width),
@@ -173,10 +177,30 @@
         out_specs=full(NC, width + 8, width),
         scratch_shapes=[pltpu.VMEM((width, width), BF16)] + [wide] * 8 + [pltpu.VMEM((rows, width), BF16)]
         + [wide] * 4 + [pltpu.VMEM((2, width, width), F32), pltpu.VMEM((walkers, 8, width), F32)],
-        compiler_params=pltpu.CompilerParams(vmem_limit_bytes=48 * 1024 * 1024),
+        compiler_params=pltpu.CompilerParams(vmem_limit_bytes=60 * 1024 * 1024),
         name="local_part",
     )(cot, tangent0.reshape(-1, width), hidden0.reshape(rows, width), laplace0.reshape(rows, width),
-      spins.reshape(rows, 1), weights, spin_bias, readout.reshape(1, width))
+      spins, weights, spin_bias, readout.reshape(1, width))
+
+
+def last_sum_kernel(parts_ref, own_ref, energy_ref, weights_ref, bias_ref, read_ref):
+    total = jnp.sum(parts_ref[...], axis=0)
+    block = weights_ref.shape[1]
+    for l in range(2):
+        weights_ref[l] = total[l * block:(l + 1) * block]
+        bias_ref[l] = total[2 * (block + l):2 * (block + l) + 2]
+    read_ref[...] = total[2 * block + 4]
+    energy_ref[...] = own_ref[2 * block + 5, :energy_ref.shape[0]]
+
+
+def last_sum(parts, own, walkers):
+    width = parts.shape[-1]
+    shapes = ((walkers,), (2, width // GROUP, width), (2, 2, width), (width,))
+    return pl.pallas_call(
+        last_sum_kernel,
+        out_shape=[jax.ShapeDtypeStruct(s, F32) for s in shapes],
+        name="last_sum",
+    )(parts, own)
 
 
 def per_device(hidden0, tangent0, laplace0, spins, weights, spin_bias, readout, energy_cotangent):
@@ -188,13 +212,11 @@
     tail = jnp.broadcast_to(part[None, width:], (NY, 8, width))
     part = jnp.concatenate([part[:width].reshape(NY, block, width), tail], axis=1)
     part = jnp.sum(lax.all_to_all(part, "y", 0, 0), axis=0)
-    energy = part[block + 5, :walkers]
-    for axis, size in (("x", NX), ("z", NZ)):
-        part = jnp.broadcast_to(part[None], (size,) + part.shape)
-        part = jnp.sum(lax.all_to_all(part, axis, 0, 0), axis=0)
-    grad_weights = part[:block].reshape(2, block // 2, width)
-    grad_bias = part[block:block + 4].reshape(2, 2, width)
-    return energy, grad_weights, grad_bias, part[block + 4]
+    own = part
+    part = jnp.broadcast_to(part[None], (NX,) + part.shape)
+    part = jnp.sum(lax.all_to_all(part, "x", 0, 0), axis=0)
+    part = jnp.broadcast_to(part[None], (NZ,) + part.shape)
+    return last_sum(lax.all_to_all(part, "z", 0, 0), own, walkers)
 
 
 def solution(mesh):

time: 77 us -> 69.4 us (0.901)
  the two profiles are of different devices: /device:TPU:8 before, /device:TPU:2 now
where the time goes in v2:
time: 69.4 us; the launch traced here: 69.1 us
  blocking collectives  56.4 us (81%)
  Pallas kernels  11.8 us (17%)
  between operations  0.7 us (1%)
    all_to_all x1, blocking collectives, per_device(): return last_sum(lax.all_to_all(part, 'z', 0, 0), own, walkers)  21.4 us
    all_to_all x1, blocking collectives, per_device(): part = jnp.sum(lax.all_to_all(part, 'y', 0, 0), axis=0)  20.5 us
    pallas_call x1, Pallas kernels, local_part(): pl.pallas_call(body, grid=(walkers, steps), out_shape=jax.ShapeDtypeStruc...  10.2 us
    all_to_all x1, blocking collectives, per_device(): part = jnp.sum(lax.all_to_all(part, 'x', 0, 0), axis=0)  9.32 us
    all_to_all x1, blocking collectives, per_device(): part = jnp.sum(lax.all_to_all(part, 'core', 0, 0), axis=0)  5.23 us
    pallas_call x1, Pallas kernels, last_sum(): pl.pallas_call(last_sum_kernel, out_shape=[jax.ShapeDtypeStruct(s, F32) f...  1.61 us

profile of v2, /device:TPU:2, one launch (start us, length us, event | category | flops | bytes accessed | tf_op | source)
XLA Modules:
  0.0 69.1 jit_solution(14894242337274875511)
XLA Ops:
  0.6 10.2 %local_part.1 = f32[2,264,256]{2,1,0:T(8,128)} custom-call(f32[2]{0:T(128)} %cot_ref.1, bf16[3840,256]{1,0:T(8,128)(2,1)} %bitcast.5, f32[240,256]{1,0:T(8,128)} %bitcast.7, f32[240,256]{1,0:T(8,128)} %bitcast.8, s32[2,120]{1,0:T(2,128)} %spin_ref.1, bf16[2,256,256]{2,1,0:T(8,128)(2,1)} %w_ref.1, f32[2,2,256]{2,1,0:T(2,128)} %bias_ref.1, f32[1,256]{1,0:T(1,128)} %bitcast.9), custom_call_target="tpu_custom_call" | custom-call | tf_op jit(solution)/shard_map/local_part/pallas_call | solution.py:163
  10.8 5.2 %all_to_all.20 = f32[2,264,256]{2,1,0:T(8,128)S(1)} all-to-all(f32[2,264,256]{2,1,0:T(8,128)} %local_part.1), channel_id=1, replica_groups=mesh['x'=4,'z'=8,'y'=8,'core'=2] {'core'}, dimensions={0} | all-to-all | bytes 1081344 | tf_op jit(solution)/shard_map/all_to_all | solution.py:211
  16.1 20.5 %all_to_all.21 = f32[8,40,256]{2,1,0:T(8,128)S(1)} all-to-all(f32[8,40,256]{2,1,0:T(8,128)S(1)} %pad_maximum_fusion), channel_id=1, replica_groups=mesh['x'=4,'z'=8,'y'=8,'core'=2] {'y'}, dimensions={0} | all-to-all | bytes 655360 | tf_op jit(solution)/shard_map/all_to_all | solution.py:214
  36.7 0.0 copy-start
  36.7 9.3 %all_to_all.22 = f32[4,40,256]{2,1,0:T(8,128)S(1)} all-to-all(f32[4,40,256]{2,1,0:T(8,128)S(1)} %broadcast_in_dim.7), channel_id=1, replica_groups=mesh['x'=4,'z'=8,'y'=8,'core'=2] {'x'}, dimensions={0} | all-to-all | bytes 327680 | tf_op jit(solution)/shard_map/all_to_all | solution.py:217
  46.0 21.4 %all_to_all.23.parts_ref = f32[8,40,256]{2,1,0:T(8,128)} all-to-all(f32[8,40,256]{2,1,0:T(8,128)S(1)} %broadcast_in_dim.8), channel_id=1, replica_groups=mesh['x'=4,'z'=8,'y'=8,'core'=2] {'z'}, dimensions={0} | all-to-all | bytes 655360 | tf_op jit(solution)/shard_map/all_to_all | solution.py:219
  67.4 0.0 copy-done
  67.4 1.6 %last_sum.1 = (f32[2]{0:T(128)}, f32[2,16,256]{2,1,0:T(8,128)}, f32[2,2,256]{2,1,0:T(2,128)}, f32[256]{0:T(256)}) custom-call(f32[8,40,256]{2,1,0:T(8,128)} %all_to_all.23.parts_ref, f32[40,256]{1,0:T(8,128)} %copy-done), custom_call_target="tpu_custom_call" | custom-call | tf_op jit(solution)/shard_map/last_sum/pallas_call | solution.py:199
  (9 shorter events, 0.2 us)
Async XLA Ops:
  36.7 30.8 %copy-start = (f32[40,256]{1,0:T(8,128)}, f32[40,256]{1,0:T(8,128)S(1)}, u32[]{:S(2)}) copy-start(f32[40,256]{1,0:T(8,128)S(1)} %reduce_sum.28.own_ref) | copy-start | bytes 122884

commit v3 on v2

v3 whole, which is shorter than its diff:
```python
import functools

import jax
import jax.numpy as jnp
from jax import lax
from jax.experimental import pallas as pl
from jax.experimental.pallas import tpu as pltpu
from jax.sharding import Mesh, PartitionSpec as P

SUBS, SKEW, FINE, VLIM = 4, 1, 1, 60
NX, NZ, NY, NC = 4, 8, 8, 2
GROUP = NY * NC
F32 = jnp.float32
BF16 = jnp.bfloat16


def mm(a, b):
    return lax.dot_general(a, b, (((1,), (0,)), ((), ())), preferred_element_type=F32)


def outer(a, b):
    return lax.dot_general(a, b, (((0,), (0,)), ((), ())), preferred_element_type=F32)


def local_kernel(cot_ref, tan_ref, hid_ref, lap_ref, spin_ref, w_ref, bias_ref, read_ref, mine_ref, theirs_ref,
                 wt_ref, a0_ref, a1_ref, gl1_ref, h1_ref, s0_ref, s1_ref, amp1_ref, b1_ref, b0_ref,
                 sq0_ref, sq1_ref, x0_ref, x1_ref, gw_ref, acc_ref, *, walkers, tangents, ne, width, walkers_all):
    two = 2 * ne
    lo = ne // 16 * 16
    read = read_ref[...]

    def coeff(i):
        return cot_ref[i] * (1.0 / walkers_all)

    def spin_column():
        turned = spin_ref[...].astype(F32).T
        return jnp.concatenate([turned[:, i:i + 1] for i in range(walkers)], axis=0)

    def coeff_rows():
        return jnp.concatenate([jnp.broadcast_to(coeff(i) * read, (ne, width)) for i in range(walkers)], axis=0)

    wt_ref[...] = w_ref[1].T
    spin = spin_column()
    hid0 = hid_ref[...]

    def layer(hid, l):
        bias = jnp.where(spin == 0, bias_ref[l, 0:1, :], bias_ref[l, 1:2, :])
        return jnp.tanh(mm(hid.astype(BF16), w_ref[l]) + bias)

    def keep_twice(ref, v):
        for i in range(walkers):
            one = v[i * ne:(i + 1) * ne]
            ref[i] = jnp.concatenate([one, one], axis=0).astype(BF16)

    a0 = layer(hid0, 0)
    h1 = hid0 + a0
    a1 = layer(h1, 1)
    a0_ref[...] = a0
    a1_ref[...] = a1
    h1_ref[...] = h1.astype(BF16)
    s0 = 1.0 - a0 * a0
    s1 = 1.0 - a1 * a1
    cr = coeff_rows()
    gl2 = -0.5 * cr
    gl1 = gl2 + mm((s1 * gl2).astype(BF16), wt_ref[...])
    gl1_ref[...] = gl1
    keep_twice(s0_ref, s0)
    keep_twice(s1_ref, s1)
    keep_twice(amp1_ref, -cr * s1)
    keep_twice(b1_ref, 2.0 * cr * a1 * s1)
    keep_twice(b0_ref, -4.0 * a0 * s0 * gl1)
    gw_ref[...] = jnp.zeros_like(gw_ref)

    tangents_u = tangents // SUBS
    pairs = tangents_u // 2
    span = tangents_u * ne
    units = [(w, p) for w in range(walkers) for p in range(SUBS)]

    def split(v):
        return v.reshape(pairs, two, width)

    def flat(v):
        return v.reshape(pairs * two, width)

    def fold(v):
        half = v[:pairs // 2] + v[pairs // 2:]
        total = jnp.sum(half.astype(F32), axis=0)
        return total[:ne] + total[ne:]

    def rows_of(p, v):
        a = jnp.broadcast_to(v[2 * p:2 * p + 1], (lo, width)).astype(BF16)
        b = jnp.broadcast_to(v[2 * p + 1:2 * p + 2], (two - lo - 16, width)).astype(BF16)
        mid = jnp.concatenate([jnp.broadcast_to(v[2 * p:2 * p + 1], (ne - lo, width)),
                               jnp.broadcast_to(v[2 * p + 1:2 * p + 2], (16 - ne + lo, width))], axis=0)
        return jnp.concatenate([a, mid.astype(BF16), b], axis=0)

    def add(u, ref, v):
        w, p = units[u]
        ref[w] = v if p == 0 else ref[w] + v

    def tan0_of(u):
        return tan_ref[u * span:(u + 1) * span, :]

    n = len(units)
    z0, tan1, z1, gb, gz1, back, gz0 = ([None] * n for _ in range(7))

    def start(u):
        z0[u] = split(mm(tan0_of(u), w_ref[0]).astype(BF16))

    def first(u):
        w = units[u][0]
        add(u, sq0_ref, fold(z0[u] * z0[u]))
        tan1[u] = split(tan0_of(u)) + s0_ref[w][None] * z0[u]

    def second(u):
        z1[u] = split(mm(flat(tan1[u]), w_ref[1]).astype(BF16))

    def third(u):
        w = units[u][0]
        add(u, sq1_ref, fold(z1[u] * z1[u]))
        tan2 = tan1[u] + s1_ref[w][None] * z1[u]
        cols = jnp.sum(flat(tan2).astype(F32).reshape(tangents_u, ne, width), axis=1)
        g = jnp.sum(cols * read, axis=1, keepdims=True)
        squares = jnp.broadcast_to(jnp.sum(g * g, axis=0, keepdims=True), (1, width))
        add(u, acc_ref, jnp.concatenate([squares, jnp.sum(g * cols, axis=0, keepdims=True)], axis=0))
        gb[u] = jnp.broadcast_to(g, (tangents_u, width))

    def fourth(u):
        w = units[u][0]
        gains = jnp.stack([rows_of(p, gb[u]) for p in range(pairs)])
        add(u, x1_ref, fold(gains * z1[u]))
        gz1[u] = flat(gains * amp1_ref[w][None] + b1_ref[w][None] * z1[u])

    def fifth(u):
        back[u] = split(mm(gz1[u], wt_ref[...]).astype(BF16))

    def outer1(u):
        gw_ref[1] += outer(flat(tan1[u]), gz1[u])

    def sixth(u):
        w = units[u][0]
        pull = gb[u] * (-coeff(w) * read)
        gt1 = back[u] + jnp.stack([rows_of(p, pull) for p in range(pairs)])
        add(u, x0_ref, fold(gt1 * z0[u]))
        gz0[u] = flat(s0_ref[w][None] * gt1 + b0_ref[w][None] * z0[u])

    def outer0(u):
        gw_ref[0] += outer(tan0_of(u), gz0[u])

    stages = [(start,), (first, second), (third, fourth, fifth), (outer1, sixth), (outer0,)]
    if FINE:
        stages = [(start,), (first,), (second,), (third,), (fourth,), (fifth, outer1), (sixth,), (outer0,)]
    if SKEW:
        for tick in range(n + len(stages) - 1):
            for k in reversed(range(len(stages))):
                if 0 <= tick - k < n:
                    for f in stages[k]:
                        f(tick - k)
    else:
        for stage in stages:
            for u in range(n):
                for f in stage:
                    f(u)

    share = 1.0 / GROUP
    spin = spin_column()
    cr = coeff_rows()
    gl2 = -0.5 * cr
    a0, a1, gl1 = a0_ref[...], a1_ref[...], gl1_ref[...]
    s0 = 1.0 - a0 * a0
    s1 = 1.0 - a1 * a1
    whole = lambda ref: ref[...].reshape(walkers * ne, width)
    sq0, sq1 = whole(sq0_ref), whole(sq1_ref)
    lap0 = lap_ref[...]
    lb0 = lap0.astype(BF16)
    lz0 = mm(lb0, w_ref[0])
    lap1 = share * (lap0 + s0 * lz0) - 2.0 * a0 * s0 * sq0
    lb1 = lap1.astype(BF16)
    lz1 = mm(lb1, w_ref[1])
    lap2 = lap1 + s1 * lz1 - 2.0 * a1 * s1 * sq1
    glz1 = (s1 * gl2).astype(BF16)
    glz0 = (s0 * gl1).astype(BF16)
    gs1 = gl2 * lz1 - cr * whole(x1_ref)
    gz1 = (-2.0 * a1 * gs1 + (6.0 * a1 * a1 - 2.0) * gl2 * sq1) * s1
    gz1b = gz1.astype(BF16)
    gw_ref[1] += outer(h1_ref[...], gz1b) + outer(lb1, glz1)
    gh1 = mm(gz1b, wt_ref[...])
    gs0 = gl1 * (share * lz0) + whole(x0_ref)
    gz0 = (-2.0 * a0 * gs0 + (6.0 * a0 * a0 - 2.0) * gl1 * sq0 + gh1) * s0
    gw_ref[0] += outer(hid_ref[...].astype(BF16), gz0.astype(BF16)) + share * outer(lb0, glz0)
    lapsum = jnp.sum(lap2.reshape(walkers, ne, width), axis=1)
    small = []
    for gz in (gz0, gz1):
        for s in range(2):
            small.append(jnp.sum(jnp.where(spin == s, gz, 0.0), axis=0, keepdims=True))
    gread = jnp.zeros((1, width), F32)
    lane = lax.broadcasted_iota(jnp.int32, (1, width), 1)
    energy = jnp.zeros((1, width), F32)
    for i in range(walkers):
        gread -= coeff(i) * (0.5 * lapsum[i:i + 1] + acc_ref[i, 1:2, :])
        e = -0.5 * (jnp.sum(lapsum[i:i + 1] * read, axis=1, keepdims=True) + acc_ref[i, 0:1, :])
        energy = jnp.where(lane == i, e, energy)
    tail = jnp.concatenate(small + [gread, energy, jnp.zeros((2, width), F32)], axis=0)
    block = width // GROUP
    own = core_index()
    for ref, core in ((mine_ref, own), (theirs_ref, 1 - own)):
        for y in range(NY):
            at = pl.multiple_of((y * NC + core) * block, block)
            for l in range(2):
                ref[y, l * block:(l + 1) * block, :] = gw_ref[l, pl.ds(at, block), :]
            ref[y, 2 * block:, :] = tail


def core_index():
    return lax.axis_index("core")


def local_part(hidden0, tangent0, laplace0, spins, weights, spin_bias, readout, cot):
    walkers, tangents, ne, width = tangent0.shape
    rows = walkers * ne
    half = (NY, 2 * width // GROUP + 8, width)
    body = functools.partial(local_kernel, walkers=walkers, tangents=tangents, ne=ne, width=width,
                             walkers_all=walkers * NX * NZ)
    full = lambda *shape: pl.BlockSpec(shape, lambda w: (0,) * len(shape))
    wide = pltpu.VMEM((rows, width), F32)
    twice = pltpu.VMEM((walkers, 2 * ne, width), BF16)
    sums = pltpu.VMEM((walkers, ne, width), F32)
    return pl.pallas_call(
        body,
        grid=(1,),
        out_shape=[jax.ShapeDtypeStruct(half, F32)] * 2,
        in_specs=[
            pl.BlockSpec(memory_space=pltpu.SMEM),
            full(walkers * tangents * ne, width),
            full(rows, width),
            full(rows, width),
            full(walkers, ne),
            full(2, width, width),
            full(2, 2, width),
            full(1, width),
        ],
        out_specs=[full(*half)] * 2,
        scratch_shapes=[pltpu.VMEM((width, width), BF16)] + [wide] * 3 + [pltpu.VMEM((rows, width), BF16)]
        + [twice] * 5 + [sums] * 4 + [pltpu.VMEM((2, width, width), F32), pltpu.VMEM((walkers, 2, width), F32)],
        compiler_params=pltpu.CompilerParams(vmem_limit_bytes=VLIM * 1024 * 1024),
        name="local_part",
    )(cot, tangent0.reshape(-1, width), hidden0.reshape(rows, width), laplace0.reshape(rows, width),
      spins, weights, spin_bias, readout.reshape(1, width))


def last_sum_kernel(parts_ref, own_ref, energy_ref, weights_ref, bias_ref, read_ref):
    total = jnp.sum(parts_ref[...], axis=0)
    block = weights_ref.shape[1]
    for l in range(2):
        weights_ref[l] = total[l * block:(l + 1) * block]
        bias_ref[l] = total[2 * (block + l):2 * (block + l) + 2]
    read_ref[...] = total[2 * block + 4]
    energy_ref[...] = own_ref[2 * block + 5, :energy_ref.shape[0]]


def last_sum(parts, own, walkers):
    width = parts.shape[-1]
    shapes = ((walkers,), (2, width // GROUP, width), (2, 2, width), (width,))
    return pl.pallas_call(
        last_sum_kernel,
        out_shape=[jax.ShapeDtypeStruct(s, F32) for s in shapes],
        name="last_sum",
    )(parts, own)


def per_device(hidden0, tangent0, laplace0, spins, weights, spin_bias, readout, energy_cotangent):
    walkers = hidden0.shape[0]
    width = weights.shape[1]
    mine, theirs = local_part(hidden0, tangent0, laplace0, spins, weights, spin_bias, readout, energy_cotangent)
    part = mine + lax.ppermute(theirs, "core", [(0, 1), (1, 0)])
    part = jnp.sum(lax.all_to_all(part, "y", 0, 0), axis=0)
    own = part
    part = jnp.broadcast_to(part[None], (NX,) + part.shape)
    part = jnp.sum(lax.all_to_all(part, "x", 0, 0), axis=0)
    part = jnp.broadcast_to(part[None], (NZ,) + part.shape)
    return last_sum(lax.all_to_all(part, "z", 0, 0), own, walkers)


def solution(mesh):
    split = Mesh(mesh.devices.reshape(NX, NZ, NY, NC), ("x", "z", "y", "core"))
    walker, tangent = ("x", "z"), ("y", "core")
    in_specs = (
        P(walker, None, None),
        P(walker, tangent, None, None),
        P(walker, None, None),
        P(walker, None),
        P(),
        P(),
        P(),
        P(walker),
    )
    out_specs = (P(walker), P(None, tangent, None), P(), P())
    return jax.shard_map(
        per_device, mesh=split, in_specs=in_specs, out_specs=out_specs, check_vma=False
    )
```

time: 69.4 us -> 65.9 us (0.950)
  blocking collectives: 56.4 us -> 51.2 us
  Pallas kernels: 11.8 us -> 8.87 us
  starting transfers between devices: 0 us -> 1.91 us
  waiting for transfers between devices: 0 us -> 1.81 us
  other arithmetic: 0.09 us -> 1.05 us
    all_to_all x1 -> x0, blocking collectives: 5.23 us -> none  [per_device(): part = jnp.sum(lax.all_to_all(part, 'core', 0, 0), axis=0)]
    pallas_call x1, Pallas kernels: 10.2 us -> 7.26 us  [local_part(): pl.pallas_call(body, grid=(1,), out_shape=[jax.ShapeDtypeStruct(half, F32...]
    ppermute x0 -> x1, starting transfers between devices: none -> 1.91 us  [per_device(): part = mine + lax.ppermute(theirs, 'core', [(0, 1), (1, 0)])]
    ppermute x0 -> x1, waiting for transfers between devices: none -> 1.81 us  [per_device(): part = mine + lax.ppermute(theirs, 'core', [(0, 1), (1, 0)])]
    add x0 -> x1, other arithmetic: none -> 1.02 us  [per_device(): part = mine + lax.ppermute(theirs, 'core', [(0, 1), (1, 0)])]
  transfers between devices with their start and end apart: 0 -> 1, of which waited for: 0 -> 1; matrix products, arithmetic and copies ran while one was open for 0% -> 0% of each run, Pallas kernels for 0% -> 0%
where the time goes in v3:
time: 65.9 us; the launch traced here: 65.6 us
  blocking collectives  51.2 us (78%)
  Pallas kernels  8.87 us (13%)
  starting transfers between devices  1.91 us (3%)
  waiting for transfers between devices  1.81 us (3%)
  other arithmetic  1.05 us (2%)
  between operations  0.68 us (1%)
    all_to_all x1, blocking collectives, per_device(): return last_sum(lax.all_to_all(part, 'z', 0, 0), own, walkers)  21.4 us
    all_to_all x1, blocking collectives, per_device(): part = jnp.sum(lax.all_to_all(part, 'y', 0, 0), axis=0)  20.5 us
    all_to_all x1, blocking collectives, per_device(): part = jnp.sum(lax.all_to_all(part, 'x', 0, 0), axis=0)  9.32 us
    pallas_call x1, Pallas kernels, local_part(): pl.pallas_call(body, grid=(1,), out_shape=[jax.ShapeDtypeStruct(half, F32...  7.26 us
    ppermute x1, starting transfers between devices, per_device(): part = mine + lax.ppermute(theirs, 'core', [(0, 1), (1, 0)])  1.91 us
    ppermute x1, waiting for transfers between devices, per_device(): part = mine + lax.ppermute(theirs, 'core', [(0, 1), (1, 0)])  1.81 us
    pallas_call x1, Pallas kernels, last_sum(): pl.pallas_call(last_sum_kernel, out_shape=[jax.ShapeDtypeStruct(s, F32) f...  1.61 us
  transfers between devices with their start and end apart: 1, of which 1 were waited for; matrix products, arithmetic and copies ran while one was open for 0% of the time, Pallas kernels for 0%

profile of v3, /device:TPU:2, one launch (start us, length us, event | category | flops | bytes accessed | tf_op | source)
XLA Modules:
  0.0 65.6 jit_solution(3717121871092830228)
XLA Ops:
  0.6 7.3 %local_part.1 = (f32[8,40,256]{2,1,0:T(8,128)}, f32[8,40,256]{2,1,0:T(8,128)}) custom-call(f32[2]{0:T(128)} %cot_ref.1, bf16[3840,256]{1,0:T(8,128)(2,1)} %bitcast.4, f32[240,256]{1,0:T(8,128)} %bitcast.5, f32[240,256]{1,0:T(8,128)} %bitcast.6, s32[2,120]{1,0:T(2,128)} %spin_ref.1, bf16[2,256,256]{2,1,0:T(8,128)(2,1)} %w_ref.1, f32[2,2,256]{2,1,0:T(2,128)} %bias_ref.1, ...), custom_call_target="tpu_custom_call" | custom-call | tf_op jit(solution)/shard_map/local_part/pallas_call | solution.py:228
  7.9 1.9 %collective-permute-start = (f32[8,40,256]{2,1,0:T(8,128)}, f32[8,40,256]{2,1,0:T(8,128)S(1)}, u32[]{:S(2)}, u32[]{:S(2)}) collective-permute-start(f32[8,40,256]{2,1,0:T(8,128)} %get-tuple-element.7), channel_id=1, source_target_pairs={{0,1},{1,0},{2,3},{3,2},{4,5},{5,4},{6,7},{7,6},{8,9},{9,8},{10,11... | collective-permute-start | bytes 983048 | tf_op jit(solution)/shard_map/ppermute | solution.py:275
  9.8 1.8 %collective-permute-done = f32[8,40,256]{2,1,0:T(8,128)S(1)} collective-permute-done((f32[8,40,256]{2,1,0:T(8,128)}, f32[8,40,256]{2,1,0:T(8,128)S(1)}, u32[]{:S(2)}, u32[]{:S(2)}) %collective-permute-start) | collective-permute-done | bytes 327712 | tf_op jit(solution)/shard_map/ppermute | solution.py:275
  11.6 1.0 %add.3 = f32[8,40,256]{2,1,0:T(8,128)S(1)} add(f32[8,40,256]{2,1,0:T(8,128)} %get-tuple-element.6, f32[8,40,256]{2,1,0:T(8,128)S(1)} %collective-permute-done) | non-fusion elementwise | flops 81920 | bytes 983040 | tf_op jit(solution)/shard_map/add | solution.py:275
  12.6 20.5 %all_to_all.15 = f32[8,40,256]{2,1,0:T(8,128)S(1)} all-to-all(f32[8,40,256]{2,1,0:T(8,128)S(1)} %add.3), channel_id=1, replica_groups=mesh['x'=4,'z'=8,'y'=8,'core'=2] {'y'}, dimensions={0} | all-to-all | bytes 655360 | tf_op jit(solution)/shard_map/all_to_all | solution.py:276
  33.1 0.0 copy-start
  33.2 9.3 %all_to_all.16 = f32[4,40,256]{2,1,0:T(8,128)S(1)} all-to-all(f32[4,40,256]{2,1,0:T(8,128)S(1)} %broadcast_in_dim.4), channel_id=1, replica_groups=mesh['x'=4,'z'=8,'y'=8,'core'=2] {'x'}, dimensions={0} | all-to-all | bytes 327680 | tf_op jit(solution)/shard_map/all_to_all | solution.py:279
  42.5 21.4 %all_to_all.17.parts_ref = f32[8,40,256]{2,1,0:T(8,128)} all-to-all(f32[8,40,256]{2,1,0:T(8,128)S(1)} %broadcast_in_dim.5), channel_id=1, replica_groups=mesh['x'=4,'z'=8,'y'=8,'core'=2] {'z'}, dimensions={0} | all-to-all | bytes 655360 | tf_op jit(solution)/shard_map/all_to_all | solution.py:281
  63.9 0.0 copy-done
  64.0 1.6 %last_sum.1 = (f32[2]{0:T(128)}, f32[2,16,256]{2,1,0:T(8,128)}, f32[2,2,256]{2,1,0:T(2,128)}, f32[256]{0:T(256)}) custom-call(f32[8,40,256]{2,1,0:T(8,128)} %all_to_all.17.parts_ref, f32[40,256]{1,0:T(8,128)} %copy-done), custom_call_target="tpu_custom_call" | custom-call | tf_op jit(solution)/shard_map/last_sum/pallas_call | solution.py:264
  (4 shorter events, 0.1 us)
Async XLA Ops:
  7.9 3.7 %collective-permute-start = (f32[8,40,256]{2,1,0:T(8,128)}, f32[8,40,256]{2,1,0:T(8,128)S(1)}, u32[]{:S(2)}, u32[]{:S(2)}) collective-permute-start(f32[8,40,256]{2,1,0:T(8,128)} %get-tuple-element.7), channel_id=1, source_target_pairs={{0,1},{1,0},{2,3},{3,2},{4,5},{5,4},{6,7},{7,6},{8,9},{9,8},{10,11... | collective-permute-start | bytes 983048 | tf_op jit(solution)/shard_map/ppermute | solution.py:275
  33.1 30.8 %copy-start = (f32[40,256]{1,0:T(8,128)}, f32[40,256]{1,0:T(8,128)S(1)}, u32[]{:S(2)}) copy-start(f32[40,256]{1,0:T(8,128)S(1)} %reduce_sum.18.own_ref) | copy-start | bytes 122884

commit v4 on v3

--- a/solution.py
+++ b/solution.py
@@ -10,6 +10,8 @@
 SUBS, SKEW, FINE, VLIM = 4, 1, 1, 60
 NX, NZ, NY, NC = 4, 8, 8, 2
 GROUP = NY * NC
+LANES, HALF = 128, 64
+PIECE = 19
 F32 = jnp.float32
 BF16 = jnp.bfloat16
 
@@ -194,21 +196,48 @@
         for s in range(2):
             small.append(jnp.sum(jnp.where(spin == s, gz, 0.0), axis=0, keepdims=True))
     gread = jnp.zeros((1, width), F32)
-    lane = lax.broadcasted_iota(jnp.int32, (1, width), 1)
-    energy = jnp.zeros((1, width), F32)
+    energy = []
     for i in range(walkers):
         gread -= coeff(i) * (0.5 * lapsum[i:i + 1] + acc_ref[i, 1:2, :])
-        e = -0.5 * (jnp.sum(lapsum[i:i + 1] * read, axis=1, keepdims=True) + acc_ref[i, 0:1, :])
-        energy = jnp.where(lane == i, e, energy)
-    tail = jnp.concatenate(small + [gread, energy, jnp.zeros((2, width), F32)], axis=0)
+        energy.append(-0.5 * (jnp.sum(lapsum[i:i + 1] * read, axis=1, keepdims=True) + acc_ref[i, 0:1, 0:1]))
+    lane = lax.broadcasted_iota(jnp.int32, (1, LANES), 1)
+    here = HALF + walkers * x_index()
+    slots = jnp.zeros((1, LANES), F32)
+    for i in range(walkers):
+        slots = jnp.where(lane == here + i, energy[i], slots)
+    extras = [small_part(small + [gread], q, slots, lane) for q in range(NX)]
     block = width // GROUP
     own = core_index()
-    for ref, core in ((mine_ref, own), (theirs_ref, 1 - own)):
+    for ref, core, sign in ((mine_ref, own, -1.0), (theirs_ref, 1 - own, 1.0)):
         for y in range(NY):
             at = pl.multiple_of((y * NC + core) * block, block)
-            for l in range(2):
-                ref[y, l * block:(l + 1) * block, :] = gw_ref[l, pl.ds(at, block), :]
-            ref[y, 2 * block:, :] = tail
+            for q in range(NX):
+                l, sub = divmod(q, 2)
+                rows_q = sign * gw_ref[l, pl.ds(at + 8 * sub, 8), :]
+                base = PIECE * (y * NX + q)
+                ref[base:base + 8, :] = rows_q[:, :LANES]
+                ref[base + 8:base + 16, :] = rows_q[:, LANES:]
+                ref[base + 16:base + PIECE, :] = sign * extras[q]
+
+
+def small_part(small, q, slots, lane):
+    half, sub = divmod(q, 2)
+
+    def low(r):
+        v = small[r][:, half * LANES:(half + 1) * LANES]
+        return pltpu.roll(v, HALF, 1) if sub else v
+
+    def high(r):
+        v = small[r][:, half * LANES:(half + 1) * LANES]
+        return v if sub else pltpu.roll(v, HALF, 1)
+
+    first = lane < HALF
+    return jnp.concatenate([jnp.where(first, low(0), high(1)), jnp.where(first, low(2), high(3)),
+                            jnp.where(first, low(4), slots)], axis=0)
+
+
+def x_index():
+    return lax.axis_index("x")
 
 
 def core_index():
@@ -218,7 +247,7 @@
 def local_part(hidden0, tangent0, laplace0, spins, weights, spin_bias, readout, cot):
     walkers, tangents, ne, width = tangent0.shape
     rows = walkers * ne
-    half = (NY, 2 * width // GROUP + 8, width)
+    half = (NY * NX * PIECE, LANES)
     body = functools.partial(local_kernel, walkers=walkers, tangents=tangents, ne=ne, width=width,
                              walkers_all=walkers * NX * NZ)
     full = lambda *shape: pl.BlockSpec(shape, lambda w: (0,) * len(shape))
@@ -249,36 +278,60 @@
 
 
 def last_sum_kernel(parts_ref, own_ref, energy_ref, weights_ref, bias_ref, read_ref):
-    total = jnp.sum(parts_ref[...], axis=0)
-    block = weights_ref.shape[1]
+    walkers = energy_ref.shape[0]
+    totals = []
+    for q in range(NX):
+        pieces = [parts_ref[PIECE * (q * NZ + z):PIECE * (q * NZ + z + 1), :] for z in range(NZ)]
+        total = sum(pieces[1:], pieces[0])
+        l, sub = divmod(q, 2)
+        weights_ref[l, 8 * sub:8 * sub + 8, :LANES] = total[:8]
+        weights_ref[l, 8 * sub:8 * sub + 8, LANES:] = total[8:16]
+        totals.append(total[16:])
+    lane = lax.broadcasted_iota(jnp.int32, (1, LANES), 1)
+    first = lane < HALF
+
+    def small_row(r):
+        at = slice(r // 2, r // 2 + 1)
+        halves = []
+        for half in range(2):
+            a, b = totals[2 * half][at], totals[2 * half + 1][at]
+            if r % 2 == 0:
+                b = pltpu.roll(b, HALF, 1)
+            else:
+                a = pltpu.roll(a, HALF, 1)
+            halves.append(jnp.where(first, a, b))
+        return jnp.concatenate(halves, axis=1)
+
     for l in range(2):
-        weights_ref[l] = total[l * block:(l + 1) * block]
-        bias_ref[l] = total[2 * (block + l):2 * (block + l) + 2]
-    read_ref[...] = total[2 * block + 4]
-    energy_ref[...] = own_ref[2 * block + 5, :energy_ref.shape[0]]
-
-
-def last_sum(parts, own, walkers):
-    width = parts.shape[-1]
+        bias_ref[l] = jnp.concatenate([small_row(2 * l), small_row(2 * l + 1)], axis=0)
+    read_ref[...] = small_row(4)[0]
+    slots = own_ref[PIECE - 1:PIECE, :]
+    here = HALF + walkers * x_index()
+    spread = jnp.zeros((1, LANES), F32)
+    for i in range(walkers):
+        one = jnp.sum(jnp.where(lane == here + i, slots, 0.0), axis=1, keepdims=True)
+        spread = jnp.where(lane == i, one, spread)
+    energy_ref[...] = spread[0, :walkers]
+
+
+def last_sum(parts, own, walkers, width):
     shapes = ((walkers,), (2, width // GROUP, width), (2, 2, width), (width,))
     return pl.pallas_call(
         last_sum_kernel,
         out_shape=[jax.ShapeDtypeStruct(s, F32) for s in shapes],
         name="last_sum",
-    )(parts, own)
+    )(parts.reshape(-1, LANES), own.reshape(PIECE, LANES))
 
 
 def per_device(hidden0, tangent0, laplace0, spins, weights, spin_bias, readout, energy_cotangent):
     walkers = hidden0.shape[0]
     width = weights.shape[1]
-    mine, theirs = local_part(hidden0, tangent0, laplace0, spins, weights, spin_bias, readout, energy_cotangent)
-    part = mine + lax.ppermute(theirs, "core", [(0, 1), (1, 0)])
-    part = jnp.sum(lax.all_to_all(part, "y", 0, 0), axis=0)
-    own = part
-    part = jnp.broadcast_to(part[None], (NX,) + part.shape)
-    part = jnp.sum(lax.all_to_all(part, "x", 0, 0), axis=0)
-    part = jnp.broadcast_to(part[None], (NZ,) + part.shape)
-    return last_sum(lax.all_to_all(part, "z", 0, 0), own, walkers)
+    minus, theirs = local_part(hidden0, tangent0, laplace0, spins, weights, spin_bias, readout, energy_cotangent)
+    got = lax.ppermute(theirs, "core", [(0, 1), (1, 0)])
+    part = (lax.optimization_barrier(-minus) + got).reshape(NY * NX, PIECE, 1, LANES)
+    own = jnp.sum(lax.all_to_all(part, ("y", "x"), 0, 0), axis=0)
+    part = jnp.broadcast_to(own[None], (NX * NZ,) + own.shape)
+    return last_sum(lax.all_to_all(part, ("x", "z"), 0, 0), own, walkers, width)
 
 
 def solution(mesh):

time: 65.9 us -> 61.2 us (0.929)
  the two profiles are of different devices: /device:TPU:2 before, /device:TPU:64 now
where the time goes in v4:
time: 61.2 us; the launch traced here: 60.9 us
  blocking collectives  47.2 us (77%)
  Pallas kernels  8.96 us (15%)
  starting transfers between devices  1.91 us (3%)
  other arithmetic  1.21 us (2%)
  waiting for transfers between devices  0.79 us (1%)
  between operations  0.67 us (1%)
    all_to_all x1, blocking collectives, per_device(): own = jnp.sum(lax.all_to_all(part, ('y', 'x'), 0, 0), axis=0)  24 us
    all_to_all x1, blocking collectives, per_device(): return last_sum(lax.all_to_all(part, ('x', 'z'), 0, 0), own, walkers, width)  23.2 us
    pallas_call x1, Pallas kernels, local_part(): pl.pallas_call(body, grid=(1,), out_shape=[jax.ShapeDtypeStruct(half, F32...  7.28 us
    ppermute x1, starting transfers between devices, per_device(): got = lax.ppermute(theirs, 'core', [(0, 1), (1, 0)])  1.91 us
    pallas_call x1, Pallas kernels, last_sum(): pl.pallas_call(last_sum_kernel, out_shape=[jax.ShapeDtypeStruct(s, F32) f...  1.68 us
  transfers between devices with their start and end apart: 1, of which 1 were waited for; matrix products, arithmetic and copies ran while one was open for 2% of the time, Pallas kernels for 0%

profile of v4, /device:TPU:64, one launch (start us, length us, event | category | flops | bytes accessed | tf_op | source)
XLA Modules:
  0.0 60.9 jit_solution(14680448212987036909)
XLA Ops:
  0.6 7.3 %local_part.1 = (f32[608,128]{1,0:T(8,128)}, f32[608,128]{1,0:T(8,128)}) custom-call(f32[2]{0:T(128)} %cot_ref.1, bf16[3840,256]{1,0:T(8,128)(2,1)} %bitcast.6, f32[240,256]{1,0:T(8,128)} %bitcast.9, f32[240,256]{1,0:T(8,128)} %bitcast.10, s32[2,120]{1,0:T(2,128)} %spin_ref.1, bf16[2,256,256]{2,1,0:T(8,128)(2,1)} %w_ref.1, f32[2,2,256]{2,1,0:T(2,128)} %bias_ref.1, ...), custom_call_target="tpu_custom_call" | custom-call | tf_op jit(solution)/shard_map/local_part/pallas_call | solution.py:257
  7.9 1.9 %collective-permute-start = (f32[608,128]{1,0:T(8,128)}, f32[608,128]{1,0:T(8,128)S(1)}, u32[]{:S(2)}, u32[]{:S(2)}) collective-permute-start(f32[608,128]{1,0:T(8,128)} %get-tuple-element.7), channel_id=1, source_target_pairs={{0,1},{1,0},{2,3},{3,2},{4,5},{5,4},{6,7},{7,6},{8,9},{9,8},{10,11... | collective-permute-start | bytes 933896 | tf_op jit(solution)/shard_map/ppermute | solution.py:330
  9.8 1.0 %neg.3 = f32[608,128]{1,0:T(8,128)S(1)} negate(f32[608,128]{1,0:T(8,128)} %get-tuple-element.6) | non-fusion elementwise | flops 77824 | bytes 622592 | tf_op jit(solution)/shard_map/neg | solution.py:331
  10.8 0.8 %collective-permute-done = f32[608,128]{1,0:T(8,128)S(1)} collective-permute-done((f32[608,128]{1,0:T(8,128)}, f32[608,128]{1,0:T(8,128)S(1)}, u32[]{:S(2)}, u32[]{:S(2)}) %collective-permute-start) | collective-permute-done | bytes 311328 | tf_op jit(solution)/shard_map/ppermute | solution.py:330
  11.6 24.0 %all_to_all.10 = f32[32,19,1,128]{3,2,1,0:T(1,128)S(1)} all-to-all(f32[32,19,1,128]{3,2,1,0:T(1,128)S(1)} %bitcast.8), channel_id=1, replica_groups=mesh['x'=4,'z'=8,'y'=8,'core'=2] {'y','x'}, dimensions={0} | all-to-all | bytes 622592 | tf_op jit(solution)/shard_map/all_to_all | solution.py:332
  35.7 0.2 reduce_sum.9.own_ref
  35.9 0.0 copy-start
  35.9 0.2 broadcast_in_dim.2
  36.0 23.2 %all_to_all.11 = f32[32,19,1,128]{3,2,1,0:T(1,128)} all-to-all(f32[32,19,1,128]{3,2,1,0:T(1,128)S(1)} %broadcast_in_dim.2), channel_id=1, replica_groups=mesh['x'=4,'z'=8,'y'=8,'core'=2] {'x','z'}, dimensions={0} | all-to-all | bytes 622592 | tf_op jit(solution)/shard_map/all_to_all | solution.py:334
  59.2 0.0 copy-done
  59.2 1.7 %last_sum.1 = (f32[2]{0:T(128)}, f32[2,16,256]{2,1,0:T(8,128)}, f32[2,2,256]{2,1,0:T(2,128)}, f32[256]{0:T(256)}) custom-call(f32[608,128]{1,0:T(8,128)} %bitcast.7, f32[19,128]{1,0:T(8,128)} %copy-done), custom_call_target="tpu_custom_call" | custom-call | tf_op jit(solution)/shard_map/last_sum/pallas_call | solution.py:319
  (1 shorter events, 0.0 us)
Async XLA Ops:
  7.9 3.7 %collective-permute-start = (f32[608,128]{1,0:T(8,128)}, f32[608,128]{1,0:T(8,128)S(1)}, u32[]{:S(2)}, u32[]{:S(2)}) collective-permute-start(f32[608,128]{1,0:T(8,128)} %get-tuple-element.7), channel_id=1, source_target_pairs={{0,1},{1,0},{2,3},{3,2},{4,5},{5,4},{6,7},{7,6},{8,9},{9,8},{10,11... | collective-permute-start | bytes 933896 | tf_op jit(solution)/shard_map/ppermute | solution.py:330
  35.9 23.3 %copy-start = (f32[19,128]{1,0:T(8,128)}, f32[19,128]{1,0:T(8,128)S(1)}, u32[]{:S(2)}) copy-start(f32[19,128]{1,0:T(8,128)S(1)} %reduce_sum.9.own_ref) | copy-start | bytes 29188

commit v5 on v4

--- a/solution.py
+++ b/solution.py
@@ -12,6 +12,10 @@
 GROUP = NY * NC
 LANES, HALF = 128, 64
 PIECE = 19
+STRIDE = 3
+X_ORDER = (0, 2, 1, 3)
+YX_ORDER = [(STRIDE * k % NY, x) for x in X_ORDER for k in range(NY)]
+XZ_ORDER = [(x, STRIDE * k % NZ) for x in X_ORDER for k in range(NZ)]
 F32 = jnp.float32
 BF16 = jnp.bfloat16
 
@@ -209,15 +213,14 @@
     block = width // GROUP
     own = core_index()
     for ref, core, sign in ((mine_ref, own, -1.0), (theirs_ref, 1 - own, 1.0)):
-        for y in range(NY):
+        for n, (y, q) in enumerate(YX_ORDER):
             at = pl.multiple_of((y * NC + core) * block, block)
-            for q in range(NX):
-                l, sub = divmod(q, 2)
-                rows_q = sign * gw_ref[l, pl.ds(at + 8 * sub, 8), :]
-                base = PIECE * (y * NX + q)
-                ref[base:base + 8, :] = rows_q[:, :LANES]
-                ref[base + 8:base + 16, :] = rows_q[:, LANES:]
-                ref[base + 16:base + PIECE, :] = sign * extras[q]
+            l, sub = divmod(q, 2)
+            rows_q = sign * gw_ref[l, pl.ds(at + 8 * sub, 8), :]
+            base = PIECE * n
+            ref[base:base + 8, :] = rows_q[:, :LANES]
+            ref[base + 8:base + 16, :] = rows_q[:, LANES:]
+            ref[base + 16:base + PIECE, :] = sign * extras[q]
 
 
 def small_part(small, q, slots, lane):
@@ -281,7 +284,7 @@
     walkers = energy_ref.shape[0]
     totals = []
     for q in range(NX):
-        pieces = [parts_ref[PIECE * (q * NZ + z):PIECE * (q * NZ + z + 1), :] for z in range(NZ)]
+        pieces = [parts_ref[PIECE * n:PIECE * (n + 1), :] for n, (x, _) in enumerate(XZ_ORDER) if x == q]
         total = sum(pieces[1:], pieces[0])
         l, sub = divmod(q, 2)
         weights_ref[l, 8 * sub:8 * sub + 8, :LANES] = total[:8]
@@ -323,15 +326,19 @@
     )(parts.reshape(-1, LANES), own.reshape(PIECE, LANES))
 
 
+def exchange(pieces, axes, order):
+    return lax.all_to_all(pieces, axes, 0, 0, axis_index_groups=[order])
+
+
 def per_device(hidden0, tangent0, laplace0, spins, weights, spin_bias, readout, energy_cotangent):
     walkers = hidden0.shape[0]
     width = weights.shape[1]
     minus, theirs = local_part(hidden0, tangent0, laplace0, spins, weights, spin_bias, readout, energy_cotangent)
     got = lax.ppermute(theirs, "core", [(0, 1), (1, 0)])
     part = (lax.optimization_barrier(-minus) + got).reshape(NY * NX, PIECE, 1, LANES)
-    own = jnp.sum(lax.all_to_all(part, ("y", "x"), 0, 0), axis=0)
+    own = jnp.sum(exchange(part, ("y", "x"), [y * NX + x for y, x in YX_ORDER]), axis=0)
     part = jnp.broadcast_to(own[None], (NX * NZ,) + own.shape)
-    return last_sum(lax.all_to_all(part, ("x", "z"), 0, 0), own, walkers, width)
+    return last_sum(exchange(part, ("x", "z"), [x * NZ + z for x, z in XZ_ORDER]), own, walkers, width)
 
 
 def solution(mesh):

time: 61.2 us -> 61.5 us (level)
  the two profiles are of different devices: /device:TPU:64 before, /device:TPU:8 now
where the time goes in v5:
time: 61.5 us; the launch traced here: 61.2 us
  blocking collectives  47.5 us (77%)
  Pallas kernels  8.96 us (15%)
  starting transfers between devices  1.91 us (3%)
  other arithmetic  1.21 us (2%)
  waiting for transfers between devices  0.79 us (1%)
  between operations  0.67 us (1%)
    all_to_all x2, blocking collectives, exchange(): return lax.all_to_all(pieces, axes, 0, 0, axis_index_groups=[order])  47.5 us
    pallas_call x1, Pallas kernels, local_part(): pl.pallas_call(body, grid=(1,), out_shape=[jax.ShapeDtypeStruct(half, F32...  7.28 us
    ppermute x1, starting transfers between devices, per_device(): got = lax.ppermute(theirs, 'core', [(0, 1), (1, 0)])  1.91 us
    pallas_call x1, Pallas kernels, last_sum(): pl.pallas_call(last_sum_kernel, out_shape=[jax.ShapeDtypeStruct(s, F32) f...  1.68 us
  transfers between devices with their start and end apart: 1, of which 1 were waited for; matrix products, arithmetic and copies ran while one was open for 2% of the time, Pallas kernels for 0%

profile of v5, /device:TPU:8, one launch (start us, length us, event | category | flops | bytes accessed | tf_op | source)
XLA Modules:
  0.0 61.2 jit_solution(10524063464105006433)
XLA Ops:
  0.6 7.3 %local_part.1 = (f32[608,128]{1,0:T(8,128)}, f32[608,128]{1,0:T(8,128)}) custom-call(f32[2]{0:T(128)} %cot_ref.1, bf16[3840,256]{1,0:T(8,128)(2,1)} %bitcast.6, f32[240,256]{1,0:T(8,128)} %bitcast.9, f32[240,256]{1,0:T(8,128)} %bitcast.10, s32[2,120]{1,0:T(2,128)} %spin_ref.1, bf16[2,256,256]{2,1,0:T(8,128)(2,1)} %w_ref.1, f32[2,2,256]{2,1,0:T(2,128)} %bias_ref.1, ...), custom_call_target="tpu_custom_call" | custom-call | tf_op jit(solution)/shard_map/local_part/pallas_call | solution.py:260
  7.9 1.9 %collective-permute-start = (f32[608,128]{1,0:T(8,128)}, f32[608,128]{1,0:T(8,128)S(1)}, u32[]{:S(2)}, u32[]{:S(2)}) collective-permute-start(f32[608,128]{1,0:T(8,128)} %get-tuple-element.7), channel_id=1, source_target_pairs={{0,1},{1,0},{2,3},{3,2},{4,5},{5,4},{6,7},{7,6},{8,9},{9,8},{10,11... | collective-permute-start | bytes 933896 | tf_op jit(solution)/shard_map/ppermute | solution.py:337
  9.8 1.0 %neg.3 = f32[608,128]{1,0:T(8,128)S(1)} negate(f32[608,128]{1,0:T(8,128)} %get-tuple-element.6) | non-fusion elementwise | flops 77824 | bytes 622592 | tf_op jit(solution)/shard_map/neg | solution.py:338
  10.8 0.8 %collective-permute-done = f32[608,128]{1,0:T(8,128)S(1)} collective-permute-done((f32[608,128]{1,0:T(8,128)}, f32[608,128]{1,0:T(8,128)S(1)}, u32[]{:S(2)}, u32[]{:S(2)}) %collective-permute-start) | collective-permute-done | bytes 311328 | tf_op jit(solution)/shard_map/ppermute | solution.py:337
  11.6 22.3 %all_to_all.10 = f32[32,19,1,128]{3,2,1,0:T(1,128)S(1)} all-to-all(f32[32,19,1,128]{3,2,1,0:T(1,128)S(1)} %bitcast.8), channel_id=1, replica_groups={{0,6,12,2,8,14,4,10,256,262,268,258,264,270,260,266,128,134,140,130,136..., dimensions={0} | all-to-all | bytes 622592 | tf_op jit(solution)/shard_map/all_to_all | solution.py:330
  33.9 0.2 reduce_sum.9.own_ref
  34.1 0.0 copy-start
  34.1 0.2 broadcast_in_dim.2
  34.3 25.2 %all_to_all.11 = f32[32,19,1,128]{3,2,1,0:T(1,128)} all-to-all(f32[32,19,1,128]{3,2,1,0:T(1,128)S(1)} %broadcast_in_dim.2), channel_id=1, replica_groups={{0,48,96,16,64,112,32,80,256,304,352,272,320,368,288,336,128,176,224,14..., dimensions={0} | all-to-all | bytes 622592 | tf_op jit(solution)/shard_map/all_to_all | solution.py:330
  59.5 0.0 copy-done
  59.5 1.7 %last_sum.1 = (f32[2]{0:T(128)}, f32[2,16,256]{2,1,0:T(8,128)}, f32[2,2,256]{2,1,0:T(2,128)}, f32[256]{0:T(256)}) custom-call(f32[608,128]{1,0:T(8,128)} %bitcast.7, f32[19,128]{1,0:T(8,128)} %copy-done), custom_call_target="tpu_custom_call" | custom-call | tf_op jit(solution)/shard_map/last_sum/pallas_call | solution.py:322
  (1 shorter events, 0.0 us)
Async XLA Ops:
  7.9 3.7 %collective-permute-start = (f32[608,128]{1,0:T(8,128)}, f32[608,128]{1,0:T(8,128)S(1)}, u32[]{:S(2)}, u32[]{:S(2)}) collective-permute-start(f32[608,128]{1,0:T(8,128)} %get-tuple-element.7), channel_id=1, source_target_pairs={{0,1},{1,0},{2,3},{3,2},{4,5},{5,4},{6,7},{7,6},{8,9},{9,8},{10,11... | collective-permute-start | bytes 933896 | tf_op jit(solution)/shard_map/ppermute | solution.py:337
  34.1 25.4 %copy-start = (f32[19,128]{1,0:T(8,128)}, f32[19,128]{1,0:T(8,128)S(1)}, u32[]{:S(2)}) copy-start(f32[19,128]{1,0:T(8,128)S(1)} %reduce_sum.9.own_ref) | copy-start | bytes 29188

commit v6 on v5

--- a/solution.py
+++ b/solution.py
@@ -322,6 +322,7 @@
     return pl.pallas_call(
         last_sum_kernel,
         out_shape=[jax.ShapeDtypeStruct(s, F32) for s in shapes],
+        compiler_params=pltpu.CompilerParams(vmem_limit_bytes=4 * 1024 * 1024),
         name="last_sum",
     )(parts.reshape(-1, LANES), own.reshape(PIECE, LANES))
 

time: 61.5 us -> 60.4 us (0.982)
  Pallas kernels: 8.96 us -> 7.99 us
    pallas_call x1, Pallas kernels: 1.68 us -> 0.71 us  [last_sum(): pl.pallas_call(last_sum_kernel, out_shape=[jax.ShapeDtypeStruct(s, F32) f...]
where the time goes in v6:
time: 60.4 us; the launch traced here: 60.1 us
  blocking collectives  47.4 us (78%)
  Pallas kernels  7.99 us (13%)
  starting transfers between devices  1.91 us (3%)
  other arithmetic  1.21 us (2%)
  waiting for transfers between devices  0.79 us (1%)
  between operations  0.66 us (1%)
    all_to_all x2, blocking collectives, exchange(): return lax.all_to_all(pieces, axes, 0, 0, axis_index_groups=[order])  47.4 us
    pallas_call x1, Pallas kernels, local_part(): pl.pallas_call(body, grid=(1,), out_shape=[jax.ShapeDtypeStruct(half, F32...  7.28 us
    ppermute x1, starting transfers between devices, per_device(): got = lax.ppermute(theirs, 'core', [(0, 1), (1, 0)])  1.91 us
  transfers between devices with their start and end apart: 1, of which 1 were waited for; matrix products, arithmetic and copies ran while one was open for 2% of the time, Pallas kernels for 0%

profile of v6, /device:TPU:8, one launch (start us, length us, event | category | flops | bytes accessed | tf_op | source)
XLA Modules:
  0.0 60.1 jit_solution(12971675958281570360)
XLA Ops:
  0.6 7.3 %local_part.1 = (f32[608,128]{1,0:T(8,128)}, f32[608,128]{1,0:T(8,128)}) custom-call(f32[2]{0:T(128)} %cot_ref.1, bf16[3840,256]{1,0:T(8,128)(2,1)} %bitcast.7, f32[240,256]{1,0:T(8,128)} %bitcast.9, f32[240,256]{1,0:T(8,128)} %bitcast.10, s32[2,120]{1,0:T(2,128)} %spin_ref.1, bf16[2,256,256]{2,1,0:T(8,128)(2,1)} %w_ref.1, f32[2,2,256]{2,1,0:T(2,128)} %bias_ref.1, ...), custom_call_target="tpu_custom_call" | custom-call | tf_op jit(solution)/shard_map/local_part/pallas_call | solution.py:260
  7.9 1.9 %collective-permute-start = (f32[608,128]{1,0:T(8,128)}, f32[608,128]{1,0:T(8,128)S(1)}, u32[]{:S(2)}, u32[]{:S(2)}) collective-permute-start(f32[608,128]{1,0:T(8,128)} %get-tuple-element.7), channel_id=1, source_target_pairs={{0,1},{1,0},{2,3},{3,2},{4,5},{5,4},{6,7},{7,6},{8,9},{9,8},{10,11... | collective-permute-start | bytes 933896 | tf_op jit(solution)/shard_map/ppermute | solution.py:338
  9.8 1.0 %neg.3 = f32[608,128]{1,0:T(8,128)S(1)} negate(f32[608,128]{1,0:T(8,128)} %get-tuple-element.6) | non-fusion elementwise | flops 77824 | bytes 622592 | tf_op jit(solution)/shard_map/neg | solution.py:339
  10.8 0.8 %collective-permute-done = f32[608,128]{1,0:T(8,128)S(1)} collective-permute-done((f32[608,128]{1,0:T(8,128)}, f32[608,128]{1,0:T(8,128)S(1)}, u32[]{:S(2)}, u32[]{:S(2)}) %collective-permute-start) | collective-permute-done | bytes 311328 | tf_op jit(solution)/shard_map/ppermute | solution.py:338
  11.7 22.3 %all_to_all.10 = f32[32,19,1,128]{3,2,1,0:T(1,128)S(1)} all-to-all(f32[32,19,1,128]{3,2,1,0:T(1,128)S(1)} %bitcast.8), channel_id=1, replica_groups={{0,6,12,2,8,14,4,10,256,262,268,258,264,270,260,266,128,134,140,130,136..., dimensions={0} | all-to-all | bytes 622592 | tf_op jit(solution)/shard_map/all_to_all | solution.py:331
  33.9 0.2 reduce_sum.9.own_ref
  34.1 0.2 broadcast_in_dim.2
  34.3 25.1 %all_to_all.11 = f32[32,19,1,128]{3,2,1,0:T(1,128)S(1)} all-to-all(f32[32,19,1,128]{3,2,1,0:T(1,128)S(1)} %broadcast_in_dim.2), channel_id=1, replica_groups={{0,48,96,16,64,112,32,80,256,304,352,272,320,368,288,336,128,176,224,14..., dimensions={0} | all-to-all | bytes 622592 | tf_op jit(solution)/shard_map/all_to_all | solution.py:331
  59.4 0.7 %last_sum.1 = (f32[2]{0:T(128)}, f32[2,16,256]{2,1,0:T(8,128)}, f32[2,2,256]{2,1,0:T(2,128)}, f32[256]{0:T(256)}) custom-call(f32[608,128]{1,0:T(8,128)S(1)} %bitcast.6, f32[19,128]{1,0:T(8,128)S(1)} %reduce_sum.9.own_ref), custom_call_target="tpu_custom_call" | custom-call | tf_op jit(solution)/shard_map/last_sum/pallas_call | solution.py:322
  (1 shorter events, 0.0 us)
Async XLA Ops:
  7.9 3.7 %collective-permute-start = (f32[608,128]{1,0:T(8,128)}, f32[608,128]{1,0:T(8,128)S(1)}, u32[]{:S(2)}, u32[]{:S(2)}) collective-permute-start(f32[608,128]{1,0:T(8,128)} %get-tuple-element.7), channel_id=1, source_target_pairs={{0,1},{1,0},{2,3},{3,2},{4,5},{5,4},{6,7},{7,6},{8,9},{9,8},{10,11... | collective-permute-start | bytes 933896 | tf_op jit(solution)/shard_map/ppermute | solution.py:338

commit v7 on v4

--- a/solution.py
+++ b/solution.py
@@ -7,7 +7,7 @@
 from jax.experimental.pallas import tpu as pltpu
 from jax.sharding import Mesh, PartitionSpec as P
 
-SUBS, SKEW, FINE, VLIM = 4, 1, 1, 60
+SUBS = 4
 NX, NZ, NY, NC = 4, 8, 8, 2
 GROUP = NY * NC
 LANES, HALF = 128, 64
@@ -149,20 +149,12 @@
     def outer0(u):
         gw_ref[0] += outer(tan0_of(u), gz0[u])
 
-    stages = [(start,), (first, second), (third, fourth, fifth), (outer1, sixth), (outer0,)]
-    if FINE:
-        stages = [(start,), (first,), (second,), (third,), (fourth,), (fifth, outer1), (sixth,), (outer0,)]
-    if SKEW:
-        for tick in range(n + len(stages) - 1):
-            for k in reversed(range(len(stages))):
-                if 0 <= tick - k < n:
-                    for f in stages[k]:
-                        f(tick - k)
-    else:
-        for stage in stages:
-            for u in range(n):
-                for f in stage:
-                    f(u)
+    stages = [(start,), (first,), (second,), (third,), (fourth,), (fifth, outer1), (sixth,), (outer0,)]
+    for tick in range(n + len(stages) - 1):
+        for k in reversed(range(len(stages))):
+            if 0 <= tick - k < n:
+                for f in stages[k]:
+                    f(tick - k)
 
     share = 1.0 / GROUP
     spin = spin_column()
@@ -271,7 +263,7 @@
         out_specs=[full(*half)] * 2,
         scratch_shapes=[pltpu.VMEM((width, width), BF16)] + [wide] * 3 + [pltpu.VMEM((rows, width), BF16)]
         + [twice] * 5 + [sums] * 4 + [pltpu.VMEM((2, width, width), F32), pltpu.VMEM((walkers, 2, width), F32)],
-        compiler_params=pltpu.CompilerParams(vmem_limit_bytes=VLIM * 1024 * 1024),
+        compiler_params=pltpu.CompilerParams(vmem_limit_bytes=60 * 1024 * 1024),
         name="local_part",
     )(cot, tangent0.reshape(-1, width), hidden0.reshape(rows, width), laplace0.reshape(rows, width),
       spins, weights, spin_bias, readout.reshape(1, width))
@@ -319,6 +311,7 @@
     return pl.pallas_call(
         last_sum_kernel,
         out_shape=[jax.ShapeDtypeStruct(s, F32) for s in shapes],
+        compiler_params=pltpu.CompilerParams(vmem_limit_bytes=4 * 1024 * 1024),
         name="last_sum",
     )(parts.reshape(-1, LANES), own.reshape(PIECE, LANES))
 

time: 61.2 us -> 60.1 us (0.982)
  Pallas kernels: 8.96 us -> 8 us
    pallas_call x1, Pallas kernels: 1.68 us -> 0.71 us  [last_sum(): pl.pallas_call(last_sum_kernel, out_shape=[jax.ShapeDtypeStruct(s, F32) f...]
where the time goes in v7:
time: 60.1 us; the launch traced here: 59.8 us
  blocking collectives  47.1 us (78%)
  Pallas kernels  8 us (13%)
  starting transfers between devices  1.91 us (3%)
  other arithmetic  1.21 us (2%)
  waiting for transfers between devices  0.79 us (1%)
  between operations  0.66 us (1%)
    all_to_all x1, blocking collectives, per_device(): own = jnp.sum(lax.all_to_all(part, ('y', 'x'), 0, 0), axis=0)  24 us
    all_to_all x1, blocking collectives, per_device(): return last_sum(lax.all_to_all(part, ('x', 'z'), 0, 0), own, walkers, width)  23.1 us
    pallas_call x1, Pallas kernels, local_part(): pl.pallas_call(body, grid=(1,), out_shape=[jax.ShapeDtypeStruct(half, F32...  7.28 us
    ppermute x1, starting transfers between devices, per_device(): got = lax.ppermute(theirs, 'core', [(0, 1), (1, 0)])  1.91 us
  transfers between devices with their start and end apart: 1, of which 1 were waited for; matrix products, arithmetic and copies ran while one was open for 2% of the time, Pallas kernels for 0%

profile of v7, /device:TPU:64, one launch (start us, length us, event | category | flops | bytes accessed | tf_op | source)
XLA Modules:
  0.0 59.8 jit_solution(17152609577419329070)
XLA Ops:
  0.6 7.3 %local_part.1 = (f32[608,128]{1,0:T(8,128)}, f32[608,128]{1,0:T(8,128)}) custom-call(f32[2]{0:T(128)} %cot_ref.1, bf16[3840,256]{1,0:T(8,128)(2,1)} %bitcast.7, f32[240,256]{1,0:T(8,128)} %bitcast.9, f32[240,256]{1,0:T(8,128)} %bitcast.10, s32[2,120]{1,0:T(2,128)} %spin_ref.1, bf16[2,256,256]{2,1,0:T(8,128)(2,1)} %w_ref.1, f32[2,2,256]{2,1,0:T(2,128)} %bias_ref.1, ...), custom_call_target="tpu_custom_call" | custom-call | tf_op jit(solution)/shard_map/local_part/pallas_call | solution.py:249
  7.9 1.9 %collective-permute-start = (f32[608,128]{1,0:T(8,128)}, f32[608,128]{1,0:T(8,128)S(1)}, u32[]{:S(2)}, u32[]{:S(2)}) collective-permute-start(f32[608,128]{1,0:T(8,128)} %get-tuple-element.7), channel_id=1, source_target_pairs={{0,1},{1,0},{2,3},{3,2},{4,5},{5,4},{6,7},{7,6},{8,9},{9,8},{10,11... | collective-permute-start | bytes 933896 | tf_op jit(solution)/shard_map/ppermute | solution.py:323
  9.8 1.0 %neg.3 = f32[608,128]{1,0:T(8,128)S(1)} negate(f32[608,128]{1,0:T(8,128)} %get-tuple-element.6) | non-fusion elementwise | flops 77824 | bytes 622592 | tf_op jit(solution)/shard_map/neg | solution.py:324
  10.8 0.8 %collective-permute-done = f32[608,128]{1,0:T(8,128)S(1)} collective-permute-done((f32[608,128]{1,0:T(8,128)}, f32[608,128]{1,0:T(8,128)S(1)}, u32[]{:S(2)}, u32[]{:S(2)}) %collective-permute-start) | collective-permute-done | bytes 311328 | tf_op jit(solution)/shard_map/ppermute | solution.py:323
  11.7 24.0 %all_to_all.10 = f32[32,19,1,128]{3,2,1,0:T(1,128)S(1)} all-to-all(f32[32,19,1,128]{3,2,1,0:T(1,128)S(1)} %bitcast.8), channel_id=1, replica_groups=mesh['x'=4,'z'=8,'y'=8,'core'=2] {'y','x'}, dimensions={0} | all-to-all | bytes 622592 | tf_op jit(solution)/shard_map/all_to_all | solution.py:325
  35.7 0.2 reduce_sum.9.own_ref
  35.9 0.2 broadcast_in_dim.2
  36.0 23.1 %all_to_all.11 = f32[32,19,1,128]{3,2,1,0:T(1,128)S(1)} all-to-all(f32[32,19,1,128]{3,2,1,0:T(1,128)S(1)} %broadcast_in_dim.2), channel_id=1, replica_groups=mesh['x'=4,'z'=8,'y'=8,'core'=2] {'x','z'}, dimensions={0} | all-to-all | bytes 622592 | tf_op jit(solution)/shard_map/all_to_all | solution.py:327
  59.1 0.7 %last_sum.1 = (f32[2]{0:T(128)}, f32[2,16,256]{2,1,0:T(8,128)}, f32[2,2,256]{2,1,0:T(2,128)}, f32[256]{0:T(256)}) custom-call(f32[608,128]{1,0:T(8,128)S(1)} %bitcast.6, f32[19,128]{1,0:T(8,128)S(1)} %reduce_sum.9.own_ref), custom_call_target="tpu_custom_call" | custom-call | tf_op jit(solution)/shard_map/last_sum/pallas_call | solution.py:311
  (1 shorter events, 0.0 us)
Async XLA Ops:
  7.9 3.7 %collective-permute-start = (f32[608,128]{1,0:T(8,128)}, f32[608,128]{1,0:T(8,128)S(1)}, u32[]{:S(2)}, u32[]{:S(2)}) collective-permute-start(f32[608,128]{1,0:T(8,128)} %get-tuple-element.7), channel_id=1, source_target_pairs={{0,1},{1,0},{2,3},{3,2},{4,5},{5,4},{6,7},{7,6},{8,9},{9,8},{10,11... | collective-permute-start | bytes 933896 | tf_op jit(solution)/shard_map/ppermute | solution.py:323

commit v8 on v7

--- a/solution.py
+++ b/solution.py
@@ -12,6 +12,8 @@
 GROUP = NY * NC
 LANES, HALF = 128, 64
 PIECE = 19
+YX_ORDER = [(y, x) for y in range(NY) for x in range(NX)][::-1]
+XZ_ORDER = [(x, z) for x in range(NX) for z in range(NZ)][::-1]
 F32 = jnp.float32
 BF16 = jnp.bfloat16
 
@@ -201,15 +203,14 @@
     block = width // GROUP
     own = core_index()
     for ref, core, sign in ((mine_ref, own, -1.0), (theirs_ref, 1 - own, 1.0)):
-        for y in range(NY):
+        for n, (y, q) in enumerate(YX_ORDER):
             at = pl.multiple_of((y * NC + core) * block, block)
-            for q in range(NX):
-                l, sub = divmod(q, 2)
-                rows_q = sign * gw_ref[l, pl.ds(at + 8 * sub, 8), :]
-                base = PIECE * (y * NX + q)
-                ref[base:base + 8, :] = rows_q[:, :LANES]
-                ref[base + 8:base + 16, :] = rows_q[:, LANES:]
-                ref[base + 16:base + PIECE, :] = sign * extras[q]
+            l, sub = divmod(q, 2)
+            rows_q = sign * gw_ref[l, pl.ds(at + 8 * sub, 8), :]
+            base = PIECE * n
+            ref[base:base + 8, :] = rows_q[:, :LANES]
+            ref[base + 8:base + 16, :] = rows_q[:, LANES:]
+            ref[base + 16:base + PIECE, :] = sign * extras[q]
 
 
 def small_part(small, q, slots, lane):
@@ -273,7 +274,7 @@
     walkers = energy_ref.shape[0]
     totals = []
     for q in range(NX):
-        pieces = [parts_ref[PIECE * (q * NZ + z):PIECE * (q * NZ + z + 1), :] for z in range(NZ)]
+        pieces = [parts_ref[PIECE * n:PIECE * (n + 1), :] for n, (x, _) in enumerate(XZ_ORDER) if x == q]
         total = sum(pieces[1:], pieces[0])
         l, sub = divmod(q, 2)
         weights_ref[l, 8 * sub:8 * sub + 8, :LANES] = total[:8]
@@ -316,15 +317,19 @@
     )(parts.reshape(-1, LANES), own.reshape(PIECE, LANES))
 
 
+def exchange(pieces, axes, order):
+    return lax.all_to_all(pieces, axes, 0, 0, axis_index_groups=[order])
+
+
 def per_device(hidden0, tangent0, laplace0, spins, weights, spin_bias, readout, energy_cotangent):
     walkers = hidden0.shape[0]
     width = weights.shape[1]
     minus, theirs = local_part(hidden0, tangent0, laplace0, spins, weights, spin_bias, readout, energy_cotangent)
     got = lax.ppermute(theirs, "core", [(0, 1), (1, 0)])
     part = (lax.optimization_barrier(-minus) + got).reshape(NY * NX, PIECE, 1, LANES)
-    own = jnp.sum(lax.all_to_all(part, ("y", "x"), 0, 0), axis=0)
+    own = jnp.sum(exchange(part, ("y", "x"), [y * NX + x for y, x in YX_ORDER]), axis=0)
     part = jnp.broadcast_to(own[None], (NX * NZ,) + own.shape)
-    return last_sum(lax.all_to_all(part, ("x", "z"), 0, 0), own, walkers, width)
+    return last_sum(exchange(part, ("x", "z"), [x * NZ + z for x, z in XZ_ORDER]), own, walkers, width)
 
 
 def solution(mesh):

time: 60.1 us -> 56.5 us (0.940)
  the two profiles are of different devices: /device:TPU:64 before, /device:TPU:8 now
where the time goes in v8:
time: 56.5 us; the launch traced here: 56.2 us
  blocking collectives  43.5 us (77%)
  Pallas kernels  7.99 us (14%)
  starting transfers between devices  1.91 us (3%)
  other arithmetic  1.21 us (2%)
  waiting for transfers between devices  0.79 us (1%)
  between operations  0.66 us (1%)
    all_to_all x2, blocking collectives, exchange(): return lax.all_to_all(pieces, axes, 0, 0, axis_index_groups=[order])  43.5 us
    pallas_call x1, Pallas kernels, local_part(): pl.pallas_call(body, grid=(1,), out_shape=[jax.ShapeDtypeStruct(half, F32...  7.28 us
    ppermute x1, starting transfers between devices, per_device(): got = lax.ppermute(theirs, 'core', [(0, 1), (1, 0)])  1.91 us
  transfers between devices with their start and end apart: 1, of which 1 were waited for; matrix products, arithmetic and copies ran while one was open for 2% of the time, Pallas kernels for 0%

profile of v8, /device:TPU:8, one launch (start us, length us, event | category | flops | bytes accessed | tf_op | source)
XLA Modules:
  0.0 56.2 jit_solution(3668356844094504997)
XLA Ops:
  0.6 7.3 %local_part.1 = (f32[608,128]{1,0:T(8,128)}, f32[608,128]{1,0:T(8,128)}) custom-call(f32[2]{0:T(128)} %cot_ref.1, bf16[3840,256]{1,0:T(8,128)(2,1)} %bitcast.7, f32[240,256]{1,0:T(8,128)} %bitcast.9, f32[240,256]{1,0:T(8,128)} %bitcast.10, s32[2,120]{1,0:T(2,128)} %spin_ref.1, bf16[2,256,256]{2,1,0:T(8,128)(2,1)} %w_ref.1, f32[2,2,256]{2,1,0:T(2,128)} %bias_ref.1, ...), custom_call_target="tpu_custom_call" | custom-call | tf_op jit(solution)/shard_map/local_part/pallas_call | solution.py:250
  7.9 1.9 %collective-permute-start = (f32[608,128]{1,0:T(8,128)}, f32[608,128]{1,0:T(8,128)S(1)}, u32[]{:S(2)}, u32[]{:S(2)}) collective-permute-start(f32[608,128]{1,0:T(8,128)} %get-tuple-element.7), channel_id=1, source_target_pairs={{0,1},{1,0},{2,3},{3,2},{4,5},{5,4},{6,7},{7,6},{8,9},{9,8},{10,11... | collective-permute-start | bytes 933896 | tf_op jit(solution)/shard_map/ppermute | solution.py:328
  9.8 1.0 %neg.3 = f32[608,128]{1,0:T(8,128)S(1)} negate(f32[608,128]{1,0:T(8,128)} %get-tuple-element.6) | non-fusion elementwise | flops 77824 | bytes 622592 | tf_op jit(solution)/shard_map/neg | solution.py:329
  10.8 0.8 %collective-permute-done = f32[608,128]{1,0:T(8,128)S(1)} collective-permute-done((f32[608,128]{1,0:T(8,128)}, f32[608,128]{1,0:T(8,128)S(1)}, u32[]{:S(2)}, u32[]{:S(2)}) %collective-permute-start) | collective-permute-done | bytes 311328 | tf_op jit(solution)/shard_map/ppermute | solution.py:328
  11.7 21.9 %all_to_all.10 = f32[32,19,1,128]{3,2,1,0:T(1,128)S(1)} all-to-all(f32[32,19,1,128]{3,2,1,0:T(1,128)S(1)} %bitcast.8), channel_id=1, replica_groups={{398,270,142,14,396,268,140,12,394,266,138,10,392,264,136,8,390,262,134..., dimensions={0} | all-to-all | bytes 622592 | tf_op jit(solution)/shard_map/all_to_all | solution.py:321
  33.5 0.2 reduce_sum.9.own_ref
  33.7 0.2 broadcast_in_dim.2
  33.9 21.6 %all_to_all.11 = f32[32,19,1,128]{3,2,1,0:T(1,128)S(1)} all-to-all(f32[32,19,1,128]{3,2,1,0:T(1,128)S(1)} %broadcast_in_dim.2), channel_id=1, replica_groups={{496,480,464,448,432,416,400,384,368,352,336,320,304,288,272,256,240,22..., dimensions={0} | all-to-all | bytes 622592 | tf_op jit(solution)/shard_map/all_to_all | solution.py:321
  55.5 0.7 %last_sum.1 = (f32[2]{0:T(128)}, f32[2,16,256]{2,1,0:T(8,128)}, f32[2,2,256]{2,1,0:T(2,128)}, f32[256]{0:T(256)}) custom-call(f32[608,128]{1,0:T(8,128)S(1)} %bitcast.6, f32[19,128]{1,0:T(8,128)S(1)} %reduce_sum.9.own_ref), custom_call_target="tpu_custom_call" | custom-call | tf_op jit(solution)/shard_map/last_sum/pallas_call | solution.py:312
  (1 shorter events, 0.0 us)
Async XLA Ops:
  7.9 3.7 %collective-permute-start = (f32[608,128]{1,0:T(8,128)}, f32[608,128]{1,0:T(8,128)S(1)}, u32[]{:S(2)}, u32[]{:S(2)}) collective-permute-start(f32[608,128]{1,0:T(8,128)} %get-tuple-element.7), channel_id=1, source_target_pairs={{0,1},{1,0},{2,3},{3,2},{4,5},{5,4},{6,7},{7,6},{8,9},{9,8},{10,11... | collective-permute-start | bytes 933896 | tf_op jit(solution)/shard_map/ppermute | solution.py:328

commit v9 on v8

--- a/solution.py
+++ b/solution.py
@@ -12,8 +12,8 @@
 GROUP = NY * NC
 LANES, HALF = 128, 64
 PIECE = 19
-YX_ORDER = [(y, x) for y in range(NY) for x in range(NX)][::-1]
-XZ_ORDER = [(x, z) for x in range(NX) for z in range(NZ)][::-1]
+YX_ORDER = [(y, x) for x in range(NX) for y in range(NY)][::-1]
+XZ_ORDER = [(x, z) for z in range(NZ) for x in range(NX)][::-1]
 F32 = jnp.float32
 BF16 = jnp.bfloat16
 

time: 56.5 us -> 55.3 us (0.979)
  blocking collectives: 43.5 us -> 42.3 us
    all_to_all x2, blocking collectives: 43.5 us -> 42.3 us  [exchange(): return lax.all_to_all(pieces, axes, 0, 0, axis_index_groups=[order])]
where the time goes in v9:
time: 55.3 us; the launch traced here: 55 us
  blocking collectives  42.3 us (76%)
  Pallas kernels  7.99 us (14%)
  starting transfers between devices  1.91 us (3%)
  other arithmetic  1.21 us (2%)
  waiting for transfers between devices  0.79 us (1%)
  between operations  0.66 us (1%)
    all_to_all x2, blocking collectives, exchange(): return lax.all_to_all(pieces, axes, 0, 0, axis_index_groups=[order])  42.3 us
    pallas_call x1, Pallas kernels, local_part(): pl.pallas_call(body, grid=(1,), out_shape=[jax.ShapeDtypeStruct(half, F32...  7.28 us
    ppermute x1, starting transfers between devices, per_device(): got = lax.ppermute(theirs, 'core', [(0, 1), (1, 0)])  1.91 us
  transfers between devices with their start and end apart: 1, of which 1 were waited for; matrix products, arithmetic and copies ran while one was open for 2% of the time, Pallas kernels for 0%

profile of v9, /device:TPU:8, one launch (start us, length us, event | category | flops | bytes accessed | tf_op | source)
XLA Modules:
  0.0 55.0 jit_solution(8416210298052979623)
XLA Ops:
  0.6 7.3 %local_part.1 = (f32[608,128]{1,0:T(8,128)}, f32[608,128]{1,0:T(8,128)}) custom-call(f32[2]{0:T(128)} %cot_ref.1, bf16[3840,256]{1,0:T(8,128)(2,1)} %bitcast.7, f32[240,256]{1,0:T(8,128)} %bitcast.9, f32[240,256]{1,0:T(8,128)} %bitcast.10, s32[2,120]{1,0:T(2,128)} %spin_ref.1, bf16[2,256,256]{2,1,0:T(8,128)(2,1)} %w_ref.1, f32[2,2,256]{2,1,0:T(2,128)} %bias_ref.1, ...), custom_call_target="tpu_custom_call" | custom-call | tf_op jit(solution)/shard_map/local_part/pallas_call | solution.py:250
  7.9 1.9 %collective-permute-start = (f32[608,128]{1,0:T(8,128)}, f32[608,128]{1,0:T(8,128)S(1)}, u32[]{:S(2)}, u32[]{:S(2)}) collective-permute-start(f32[608,128]{1,0:T(8,128)} %get-tuple-element.7), channel_id=1, source_target_pairs={{0,1},{1,0},{2,3},{3,2},{4,5},{5,4},{6,7},{7,6},{8,9},{9,8},{10,11... | collective-permute-start | bytes 933896 | tf_op jit(solution)/shard_map/ppermute | solution.py:328
  9.8 1.0 %neg.3 = f32[608,128]{1,0:T(8,128)S(1)} negate(f32[608,128]{1,0:T(8,128)} %get-tuple-element.6) | non-fusion elementwise | flops 77824 | bytes 622592 | tf_op jit(solution)/shard_map/neg | solution.py:329
  10.8 0.8 %collective-permute-done = f32[608,128]{1,0:T(8,128)S(1)} collective-permute-done((f32[608,128]{1,0:T(8,128)}, f32[608,128]{1,0:T(8,128)S(1)}, u32[]{:S(2)}, u32[]{:S(2)}) %collective-permute-start) | collective-permute-done | bytes 311328 | tf_op jit(solution)/shard_map/ppermute | solution.py:328
  11.7 21.9 %all_to_all.10 = f32[32,19,1,128]{3,2,1,0:T(1,128)S(1)} all-to-all(f32[32,19,1,128]{3,2,1,0:T(1,128)S(1)} %bitcast.8), channel_id=1, replica_groups={{398,396,394,392,390,388,386,384,270,268,266,264,262,260,258,256,142,14..., dimensions={0} | all-to-all | bytes 622592 | tf_op jit(solution)/shard_map/all_to_all | solution.py:321
  33.5 0.2 reduce_sum.9.own_ref
  33.7 0.2 broadcast_in_dim.2
  33.9 20.4 %all_to_all.11 = f32[32,19,1,128]{3,2,1,0:T(1,128)S(1)} all-to-all(f32[32,19,1,128]{3,2,1,0:T(1,128)S(1)} %broadcast_in_dim.2), channel_id=1, replica_groups={{496,368,240,112,480,352,224,96,464,336,208,80,448,320,192,64,432,304,1..., dimensions={0} | all-to-all | bytes 622592 | tf_op jit(solution)/shard_map/all_to_all | solution.py:321
  54.3 0.7 %last_sum.1 = (f32[2]{0:T(128)}, f32[2,16,256]{2,1,0:T(8,128)}, f32[2,2,256]{2,1,0:T(2,128)}, f32[256]{0:T(256)}) custom-call(f32[608,128]{1,0:T(8,128)S(1)} %bitcast.6, f32[19,128]{1,0:T(8,128)S(1)} %reduce_sum.9.own_ref), custom_call_target="tpu_custom_call" | custom-call | tf_op jit(solution)/shard_map/last_sum/pallas_call | solution.py:312
  (1 shorter events, 0.0 us)
Async XLA Ops:
  7.9 3.7 %collective-permute-start = (f32[608,128]{1,0:T(8,128)}, f32[608,128]{1,0:T(8,128)S(1)}, u32[]{:S(2)}, u32[]{:S(2)}) collective-permute-start(f32[608,128]{1,0:T(8,128)} %get-tuple-element.7), channel_id=1, source_target_pairs={{0,1},{1,0},{2,3},{3,2},{4,5},{5,4},{6,7},{7,6},{8,9},{9,8},{10,11... | collective-permute-start | bytes 933896 | tf_op jit(solution)/shard_map/ppermute | solution.py:328
